TPU v7x, 32 devices: a whole 2x2x4 slice. The times are simulated.
32 devices in a mesh: dp: 8 (over z, x), mp: 4 (over y, core).
Axes of the slice: x: 2, y: 2, z: 4, core: 2. Of those that a mesh axis runs over, the one named last changes fastest.
Arguments:
- enc_in: bfloat16 [8, 1344, 768], P('dp', 'mp'), may hold values from -6 to 6
- dec_in: bfloat16 [8, 448, 768], P('dp', 'mp'), may hold values from -6 to 6
- dec_len: int32 [8], P('dp'), may hold values from 5 to 448, as said below
- norm_gain: bfloat16 [5, 768], replicated, may hold values from 0.5 to 1.5
- norm_shift: bfloat16 [5, 768], replicated, may hold values from -1.8 to 1.8
- qkv: bfloat16 [3, 3, 768, 768], P(None, None, None, 'mp')
- qv_bias: bfloat16 [3, 2, 768], P(None, None, 'mp'), may hold values from -1.8 to 1.8
- proj: bfloat16 [3, 768, 768], P(None, 'mp')
- out_bias: bfloat16 [5, 768], replicated, may hold values from -1.8 to 1.8
- fc1: bfloat16 [2, 768, 3072], P(None, None, 'mp')
- fc1_bias: bfloat16 [2, 3072], P(None, 'mp'), may hold values from -1.8 to 1.8
- fc2: bfloat16 [2, 3072, 768], P(None, 'mp')
- enc_cot: bfloat16 [8, 1344, 768], P('dp', 'mp'), may hold values from -6 to 6
- dec_cot: bfloat16 [8, 448, 768], P('dp', 'mp'), may hold values from -6 to 6
Outputs:
- enc_out: bfloat16 [8, 1344, 768], P('dp', 'mp')
- dec_out: bfloat16 [8, 448, 768], P('dp', 'mp')
- enc_in_grad: float32 [8, 1344, 768], P('dp', 'mp')
- dec_in_grad: float32 [8, 448, 768], P('dp', 'mp')
- norm_gain_grad: float32 [5, 768], replicated
- norm_shift_grad: float32 [5, 768], replicated
- qkv_grad: float32 [3, 3, 768, 768], P(None, None, None, 'mp')
- qv_bias_grad: float32 [3, 2, 768], P(None, None, 'mp')
- proj_grad: float32 [3, 768, 768], P(None, 'mp')
- out_bias_grad: float32 [5, 768], replicated
- fc1_grad: float32 [2, 768, 3072], P(None, None, 'mp')
- fc1_bias_grad: float32 [2, 3072], P(None, 'mp')
- fc2_grad: float32 [2, 3072, 768], P(None, 'mp')
Inputs may be any that keep to these rules, and one draw needn't show every extreme that they name: `dec_len`: among the 1 clips of each index of dp, one, which one drawn from the seed, has tokens on every index of mp; on the first index of dp that clip has exactly 448 tokens.
All inputs are finite; a program needn't handle non-finite values.
Results may differ from a plain program's by a relative error of at most 0.017.
Values may be sent and summed in bfloat16 or wider, within the bound.
A program may use at most 192 MiB of HBM per device.

v0:
```python
import jax
import jax.numpy as jnp
from jax import lax
from jax.sharding import PartitionSpec as P

HEAD = 64


epsilon = 1e-05
masked_score = -1e30


def normalize(rows_in, gain_row, shift_row):
    average = jnp.mean(rows_in, axis=-1, keepdims=True)
    centred = rows_in - average
    spread = jnp.mean(centred * centred, axis=-1, keepdims=True)
    return centred * lax.rsqrt(spread + epsilon) * gain_row + shift_row


def norm_back(rows_in, gain_row, shift_row, gradient):
    unused, pullback = jax.vjp(normalize, rows_in, gain_row, shift_row)
    return pullback(gradient)


def activate(hidden):
    return jax.nn.gelu(hidden, approximate=False)


def activate_back(hidden, gradient):
    unused, pullback = jax.vjp(activate, hidden)
    return pullback(gradient)[0]


def product(operand, weight):
    return jnp.einsum("crd,dh->crh", operand, weight, preferred_element_type=jnp.float32)


def product_back(gradient, weight):
    return jnp.einsum("crh,dh->crd", gradient, weight, preferred_element_type=jnp.float32)


def weight_grad(operand, gradient):
    return jnp.einsum("crd,crh->dh", operand, gradient, preferred_element_type=jnp.float32)


def column_sums(gradient):
    return jnp.sum(gradient, axis=(0, 1), dtype=jnp.float32)


def gather_rows(normed):
    return lax.all_gather(normed, "mp", axis=1, tiled=True)


def sum_rows(partial_value):
    return lax.psum_scatter(partial_value, "mp", scatter_dimension=1, tiled=True)


def gather_grads(gradient):
    return lax.all_gather(gradient, "mp", axis=1, tiled=True)


def sum_grads(partial_value):
    return lax.psum_scatter(partial_value, "mp", scatter_dimension=1, tiled=True)


def score_block(queries, key_rows, causal):
    row_count = queries.shape[0]
    split_query = queries.reshape(row_count, -1, HEAD)
    split_keys = key_rows.reshape(key_rows.shape[0], -1, HEAD)
    scores = jnp.einsum(
        "rhe,she->hrs", split_query, split_keys, preferred_element_type=jnp.float32
    ) * HEAD ** (-0.5)
    if causal:
        row_index = lax.broadcasted_iota(jnp.int32, scores.shape, 1)
        col_index = lax.broadcasted_iota(jnp.int32, scores.shape, 2)
        scores = jnp.where(col_index <= row_index, scores, masked_score)
    return (scores, split_query, split_keys)


def attend(queries, key_rows, values, causal):

    def one_clip(clip_block):
        query_clip, keys_clip, values_clip = clip_block
        scores, unused_query, unused_keys = score_block(query_clip, keys_clip, causal)
        highest = jnp.max(scores, axis=-1, keepdims=True)
        logsum = highest + jnp.log(jnp.sum(jnp.exp(scores - highest), axis=-1, keepdims=True))
        weights = jnp.exp(scores - logsum).astype(jnp.bfloat16)
        split_values = values_clip.reshape(values_clip.shape[0], -1, HEAD)
        mixed_out = jnp.einsum(
            "hrs,she->rhe", weights, split_values, preferred_element_type=jnp.float32
        )
        return (mixed_out.reshape(query_clip.shape).astype(jnp.bfloat16), logsum)

    return lax.map(one_clip, (queries, key_rows, values))


def attend_back(queries, key_rows, values, logsum, gradient, causal):

    def one_clip(clip_block):
        query_clip, keys_clip, values_clip, logsum_clip, grad_clip = clip_block
        scores, split_query, split_keys = score_block(query_clip, keys_clip, causal)
        weights = jnp.exp(scores - logsum_clip)
        split_values = values_clip.reshape(values_clip.shape[0], -1, HEAD)
        split_grad = grad_clip.reshape(grad_clip.shape[0], -1, HEAD)
        weight_grads = jnp.einsum(
            "rhe,she->hrs", split_grad, split_values, preferred_element_type=jnp.float32
        )
        inner_sum = jnp.sum(weights * weight_grads, axis=-1, keepdims=True)
        score_grads = (weights * (weight_grads - inner_sum)).astype(jnp.bfloat16)
        score_scale = HEAD ** (-0.5)
        query_grad = (
            jnp.einsum("hrs,she->rhe", score_grads, split_keys, preferred_element_type=jnp.float32)
            * score_scale
        )
        keys_grad = (
            jnp.einsum("hrs,rhe->she", score_grads, split_query, preferred_element_type=jnp.float32)
            * score_scale
        )
        values_grad = jnp.einsum(
            "hrs,rhe->she",
            weights.astype(jnp.bfloat16),
            split_grad,
            preferred_element_type=jnp.float32,
        )
        return tuple(
            (
                piece_grad.reshape(piece_grad.shape[0], -1).astype(jnp.bfloat16)
                for piece_grad in (query_grad, keys_grad, values_grad)
            )
        )

    return lax.map(one_clip, (queries, key_rows, values, logsum, gradient))


def encoder_forward(frames, weights):
    norm_gain, norm_shift, qkv, qv_bias, proj, out_bias, fc1, fc1_bias, fc2 = weights
    normed = normalize(frames, norm_gain[0], norm_shift[0]).astype(jnp.bfloat16)
    gathered = gather_rows(normed)
    queries = (product(gathered, qkv[0, 0]) + qv_bias[0, 0]).astype(jnp.bfloat16)
    key_rows = product(gathered, qkv[0, 1]).astype(jnp.bfloat16)
    values = (product(gathered, qkv[0, 2]) + qv_bias[0, 1]).astype(jnp.bfloat16)
    mixed_out, logsum = attend(queries, key_rows, values, False)
    middle = frames + sum_rows(product(mixed_out, proj[0])) + out_bias[0]
    gathered_two = gather_rows(normalize(middle, norm_gain[1], norm_shift[1]).astype(jnp.bfloat16))
    hidden = product(gathered_two, fc1[0]) + fc1_bias[0]
    activated = activate(hidden).astype(jnp.bfloat16)
    encoded = middle + sum_rows(product(activated, fc2[0])) + out_bias[1]
    return (
        encoded,
        (
            gathered,
            queries,
            key_rows,
            values,
            mixed_out,
            logsum,
            middle,
            gathered_two,
            hidden,
            activated,
        ),
    )


def encoder_backward(frames, saved, gradient, weights):
    norm_gain, norm_shift, qkv, qv_bias, proj, out_bias, fc1, fc1_bias, fc2 = weights
    (
        gathered,
        queries,
        key_rows,
        values,
        mixed_out,
        logsum,
        middle,
        gathered_two,
        hidden,
        activated,
    ) = saved
    branch = gather_grads(gradient.astype(jnp.bfloat16))
    fc2_grad = weight_grad(activated, branch)
    bias_mlp = column_sums(branch)
    hidden_grad = activate_back(hidden, product_back(branch, fc2[0])).astype(jnp.bfloat16)
    fc1_grad = weight_grad(gathered_two, hidden_grad)
    fc1_bias_grad = column_sums(hidden_grad)
    middle_norm, gain_one, shift_one = norm_back(
        middle, norm_gain[1], norm_shift[1], sum_grads(product_back(hidden_grad, fc1[0]))
    )
    middle_grad = gradient + middle_norm
    branch = gather_grads(middle_grad.astype(jnp.bfloat16))
    proj_grad = weight_grad(mixed_out, branch)
    bias_attend = column_sums(branch)
    mixed_grad = product_back(branch, proj[0]).astype(jnp.bfloat16)
    query_grad, key_grad, value_grad = attend_back(
        queries, key_rows, values, logsum, mixed_grad, False
    )
    qkv_grad = jnp.stack(
        [
            weight_grad(gathered, query_grad),
            weight_grad(gathered, key_grad),
            weight_grad(gathered, value_grad),
        ]
    )
    qv_grad = jnp.stack([column_sums(query_grad), column_sums(value_grad)])
    gathered_grad = (
        product_back(query_grad, qkv[0, 0])
        + product_back(key_grad, qkv[0, 1])
        + product_back(value_grad, qkv[0, 2])
    )
    frames_norm, gain_zero, shift_zero = norm_back(
        frames, norm_gain[0], norm_shift[0], sum_grads(gathered_grad)
    )
    frames_grad = middle_grad + frames_norm
    gradients = (
        qkv_grad,
        qv_grad,
        proj_grad,
        jnp.stack([bias_attend, bias_mlp]),
        fc1_grad,
        fc1_bias_grad,
        fc2_grad,
    )
    return (
        frames_grad,
        gradients,
        jnp.stack([gain_zero, gain_one]),
        jnp.stack([shift_zero, shift_one]),
    )


def decoder_forward(tokens, memory, valid_rows, weights):
    norm_gain, norm_shift, qkv, qv_bias, proj, out_bias, fc1, fc1_bias, fc2 = weights
    gathered = gather_rows(normalize(tokens, norm_gain[2], norm_shift[2]).astype(jnp.bfloat16))
    queries = (product(gathered, qkv[1, 0]) + qv_bias[1, 0]).astype(jnp.bfloat16)
    key_rows = product(gathered, qkv[1, 1]).astype(jnp.bfloat16)
    values = (product(gathered, qkv[1, 2]) + qv_bias[1, 1]).astype(jnp.bfloat16)
    mixed_out, logsum = attend(queries, key_rows, values, True)
    after_self = tokens + sum_rows(product(mixed_out, proj[1])) + out_bias[2]
    gathered_two = gather_rows(
        normalize(after_self, norm_gain[3], norm_shift[3]).astype(jnp.bfloat16)
    )
    cross_queries = (product(gathered_two, qkv[2, 0]) + qv_bias[2, 0]).astype(jnp.bfloat16)
    cross_keys = product(memory, qkv[2, 1]).astype(jnp.bfloat16)
    cross_values = (product(memory, qkv[2, 2]) + qv_bias[2, 1]).astype(jnp.bfloat16)
    cross_mixed, cross_logsum = attend(cross_queries, cross_keys, cross_values, False)
    second = after_self + sum_rows(product(cross_mixed, proj[2])) + out_bias[3]
    gathered_three = gather_rows(
        normalize(second, norm_gain[4], norm_shift[4]).astype(jnp.bfloat16)
    )
    hidden = product(gathered_three, fc1[1]) + fc1_bias[1]
    activated = activate(hidden).astype(jnp.bfloat16)
    after_mlp = second + sum_rows(product(activated, fc2[1])) + out_bias[4]
    saved = (
        gathered,
        queries,
        key_rows,
        values,
        mixed_out,
        logsum,
        after_self,
        gathered_two,
        cross_queries,
        cross_keys,
        cross_values,
        cross_mixed,
        cross_logsum,
        second,
        gathered_three,
        hidden,
        activated,
    )
    return (after_mlp * valid_rows, saved)


def decoder_backward(tokens, memory, saved, gradient, weights):
    norm_gain, norm_shift, qkv, qv_bias, proj, out_bias, fc1, fc1_bias, fc2 = weights
    (
        gathered,
        queries,
        key_rows,
        values,
        mixed_out,
        logsum,
        after_self,
        gathered_two,
        cross_queries,
        cross_keys,
        cross_values,
        cross_mixed,
        cross_logsum,
        second,
        gathered_three,
        hidden,
        activated,
    ) = saved
    branch = gather_grads(gradient.astype(jnp.bfloat16))
    fc2_grad = weight_grad(activated, branch)
    bias_mlp = column_sums(branch)
    hidden_grad = activate_back(hidden, product_back(branch, fc2[1])).astype(jnp.bfloat16)
    fc1_grad = weight_grad(gathered_three, hidden_grad)
    fc1_bias_grad = column_sums(hidden_grad)
    second_norm, gain_three, shift_three = norm_back(
        second, norm_gain[4], norm_shift[4], sum_grads(product_back(hidden_grad, fc1[1]))
    )
    second_grad = gradient + second_norm
    branch = gather_grads(second_grad.astype(jnp.bfloat16))
    cross_proj_grad = weight_grad(cross_mixed, branch)
    bias_cross = column_sums(branch)
    cross_mixed_grad = product_back(branch, proj[2]).astype(jnp.bfloat16)
    cross_query_grad, cross_key_grad, cross_value_grad = attend_back(
        cross_queries, cross_keys, cross_values, cross_logsum, cross_mixed_grad, False
    )
    cross_qkv_grad = jnp.stack(
        [
            weight_grad(gathered_two, cross_query_grad),
            weight_grad(memory, cross_key_grad),
            weight_grad(memory, cross_value_grad),
        ]
    )
    cross_qv_grad = jnp.stack([column_sums(cross_query_grad), column_sums(cross_value_grad)])
    memory_grad = sum_grads(
        product_back(cross_key_grad, qkv[2, 1]) + product_back(cross_value_grad, qkv[2, 2])
    )
    self_norm, gain_two, shift_two = norm_back(
        after_self,
        norm_gain[3],
        norm_shift[3],
        sum_grads(product_back(cross_query_grad, qkv[2, 0])),
    )
    self_grad = second_grad + self_norm
    branch = gather_grads(self_grad.astype(jnp.bfloat16))
    self_proj_grad = weight_grad(mixed_out, branch)
    bias_self = column_sums(branch)
    mixed_grad = product_back(branch, proj[1]).astype(jnp.bfloat16)
    query_grad, key_grad, value_grad = attend_back(
        queries, key_rows, values, logsum, mixed_grad, True
    )
    self_qkv_grad = jnp.stack(
        [
            weight_grad(gathered, query_grad),
            weight_grad(gathered, key_grad),
            weight_grad(gathered, value_grad),
        ]
    )
    self_qv_grad = jnp.stack([column_sums(query_grad), column_sums(value_grad)])
    gathered_grad = (
        product_back(query_grad, qkv[1, 0])
        + product_back(key_grad, qkv[1, 1])
        + product_back(value_grad, qkv[1, 2])
    )
    tokens_norm, gain_one, shift_one = norm_back(
        tokens, norm_gain[2], norm_shift[2], sum_grads(gathered_grad)
    )
    tokens_grad = self_grad + tokens_norm
    gradients = (
        jnp.stack([self_qkv_grad, cross_qkv_grad]),
        jnp.stack([self_qv_grad, cross_qv_grad]),
        jnp.stack([self_proj_grad, cross_proj_grad]),
        jnp.stack([bias_self, bias_cross, bias_mlp]),
        fc1_grad,
        fc1_bias_grad,
        fc2_grad,
    )
    return (
        tokens_grad,
        memory_grad,
        gradients,
        jnp.stack([gain_one, gain_two, gain_three]),
        jnp.stack([shift_one, shift_two, shift_three]),
    )


def on_device(
    enc_in,
    dec_in,
    dec_len,
    norm_gain,
    norm_shift,
    qkv,
    qv_bias,
    proj,
    out_bias,
    fc1,
    fc1_bias,
    fc2,
    enc_cot,
    dec_cot,
):
    weights = (
        norm_gain.astype(jnp.float32),
        norm_shift.astype(jnp.float32),
        qkv,
        qv_bias,
        proj,
        out_bias,
        fc1,
        fc1_bias,
        fc2,
    )
    frames = enc_in.astype(jnp.float32)
    tokens = dec_in.astype(jnp.float32)
    clip_count, token_count = (dec_in.shape[0], dec_in.shape[1])
    positions = lax.axis_index("mp") * token_count + lax.broadcasted_iota(
        jnp.int32, (clip_count, token_count), 1
    )
    valid_rows = (positions < dec_len[:, None]).astype(jnp.float32)[:, :, None]
    encoded, enc_saved = encoder_forward(frames, weights)
    enc_out = encoded.astype(jnp.bfloat16)
    memory = gather_rows(enc_out)
    decoded, dec_saved = decoder_forward(tokens, memory, valid_rows, weights)
    tokens_grad, memory_grad, dec_grads, dec_gains, dec_shifts = decoder_backward(
        tokens, memory, dec_saved, dec_cot.astype(jnp.float32) * valid_rows, weights
    )
    encoded_grad = enc_cot.astype(jnp.float32) + memory_grad
    frames_again, encoded_grad = lax.optimization_barrier((frames, encoded_grad))
    unused, enc_saved = encoder_forward(frames_again, weights)
    frames_grad, enc_grads, enc_gains, enc_shifts = encoder_backward(
        frames, enc_saved, encoded_grad, weights
    )
    merged = (
        jnp.concatenate([enc_grads[0][None], dec_grads[0]]),
        jnp.concatenate([enc_grads[1][None], dec_grads[1]]),
        jnp.concatenate([enc_grads[2][None], dec_grads[2]]),
        jnp.concatenate([enc_grads[3], dec_grads[3]]),
        jnp.stack([enc_grads[4], dec_grads[4]]),
        jnp.stack([enc_grads[5], dec_grads[5]]),
        jnp.stack([enc_grads[6], dec_grads[6]]),
    )
    merged = lax.psum(
        (merged[0], merged[1], merged[2], merged[3], merged[4], merged[5], merged[6]), "dp"
    )
    gain_grad, shift_grad = lax.psum(
        (jnp.concatenate([enc_gains, dec_gains]), jnp.concatenate([enc_shifts, dec_shifts])),
        ("dp", "mp"),
    )
    return (
        enc_out,
        decoded.astype(jnp.bfloat16),
        frames_grad,
        tokens_grad,
        gain_grad,
        shift_grad,
        merged[0],
        merged[1],
        merged[2],
        merged[3],
        merged[4],
        merged[5],
        merged[6],
    )


def solution(mesh):
    placed = (
        P("dp", "mp", None),
        P("dp", "mp", None),
        P("dp"),
        P(),
        P(),
        P(None, None, None, "mp"),
        P(None, None, "mp"),
        P(None, "mp", None),
        P(),
        P(None, None, "mp"),
        P(None, "mp"),
        P(None, "mp", None),
        P("dp", "mp", None),
        P("dp", "mp", None),
    )
    return jax.shard_map(
        on_device,
        mesh=mesh,
        in_specs=placed,
        out_specs=(
            P("dp", "mp", None),
            P("dp", "mp", None),
            P("dp", "mp", None),
            P("dp", "mp", None),
            P(),
            P(),
            P(None, None, None, "mp"),
            P(None, None, "mp"),
            P(None, "mp", None),
            P(),
            P(None, None, "mp"),
            P(None, "mp"),
            P(None, "mp", None),
        ),
        check_vma=False,
    )
```

profile of v0, /device:TPU:0, one launch (start us, length us, event | category | flops | bytes accessed | tf_op | source)
XLA Modules:
  0.0 1349.6 jit_solution(11558510023806839752)
XLA Ops:
  14.7 25.2 %all-gather.8.cloned.1.call-done = bf16[1,1344,768]{2,1,0:T(8,128)(2,1)} async-done(((bf16[1,336,768]{2,1,0:T(8,128)(2,1)}), bf16[1,1344,768]{2,1,0:T(8,128)(2,1)}) %all-gather.8.cloned.1.call-update) | async-done | bytes 2064400 | tf_op jit(solution)/shard_map/all_gather | solution.py:51
  72.2 43.0 %reduce-scatter.13.cloned.1.call-done = f32[1,336,768]{2,1,0:T(8,128)} async-done(((f32[1,1344,768]{2,1,0:T(8,128)}), f32[1,336,768]{2,1,0:T(8,128)}) %reduce-scatter.13.cloned.1.call-update) | async-done | bytes 1032208 | tf_op jit(solution)/shard_map/reduce_scatter | solution.py:55
  119.6 22.3 %all-gather.10.cloned.1.call-done = bf16[1,1344,768]{2,1,0:T(8,128)(2,1)} async-done(((bf16[1,336,768]{2,1,0:T(8,128)(2,1)}), bf16[1,1344,768]{2,1,0:T(8,128)(2,1)}) %all-gather.10.cloned.1.call-update) | async-done | bytes 2064400 | tf_op jit(solution)/shard_map/all_gather | solution.py:51
  141.9 15.8 %convolution_bitcast_fusion.1 = f32[1,1344,768]{2,1,0:T(8,128)} fusion(bf16[1,1344,768]{2,1,0:T(8,128)(2,1)} %all-gather.10.cloned.1.call-done, f32[768]{0:T(1024)S(1)} %get-tuple-element.200, bf16[2,768,768]{2,1,0:T(8,128)(2,1)} %param.25, bf16[2,768,768]{2,1,0:T(8,128)(2,1)} %param.23), kind=kOutput, calls=%fused_computation.63 | convolution fusion | flops 3239018496 | bytes 8555520 | tf_op jit(solution)/shard_map/crd,dh->crh/dot_general | solution.py:35
  176.7 25.3 %reduce-scatter.15.cloned.1.call-done = f32[1,336,768]{2,1,0:T(8,128)} async-done(((f32[1,1344,768]{2,1,0:T(8,128)}), f32[1,336,768]{2,1,0:T(8,128)}) %reduce-scatter.15.cloned.1.call-update) | async-done | bytes 1032208 | tf_op jit(solution)/shard_map/reduce_scatter | solution.py:55
  204.3 27.6 %reduce-scatter.17.cloned.1.call-done = f32[1,112,768]{2,1,0:T(8,128)} async-done(((f32[1,448,768]{2,1,0:T(8,128)}), f32[1,112,768]{2,1,0:T(8,128)}) %reduce-scatter.17.cloned.1.call-update) | async-done | bytes 344080 | tf_op jit(solution)/shard_map/reduce_scatter | solution.py:55
  243.4 13.1 all-gather.12.cloned.1.call-done
  278.1 18.3 %reduce-scatter.19.cloned.1.call-done = f32[1,112,768]{2,1,0:T(8,128)} async-done(((f32[1,448,768]{2,1,0:T(8,128)}), f32[1,112,768]{2,1,0:T(8,128)}) %reduce-scatter.19.cloned.1.call-update) | async-done | bytes 344080 | tf_op jit(solution)/shard_map/reduce_scatter | solution.py:55
  322.2 24.3 %reduce-scatter.23.cloned.1.call-done = f32[1,112,768]{2,1,0:T(8,128)} async-done(((f32[1,448,768]{2,1,0:T(8,128)}), f32[1,112,768]{2,1,0:T(8,128)}) %reduce-scatter.23.cloned.1.call-update) | async-done | bytes 344080 | tf_op jit(solution)/shard_map/reduce_scatter | solution.py:63
  349.5 27.3 %reduce-scatter.21.cloned.1.call-done = f32[1,112,768]{2,1,0:T(8,128)} async-done(((f32[1,448,768]{2,1,0:T(8,128)}), f32[1,112,768]{2,1,0:T(8,128)}) %reduce-scatter.21.cloned.1.call-update) | async-done | bytes 344080 | tf_op jit(solution)/shard_map/reduce_scatter | solution.py:55
  409.6 43.6 %reduce-scatter.25.cloned.1.call-done = f32[1,336,768]{2,1,0:T(8,128)} async-done(((f32[1,1344,768]{2,1,0:T(8,128)}), f32[1,336,768]{2,1,0:T(8,128)}) %reduce-scatter.25.cloned.1.call-update) | async-done | bytes 1032208 | tf_op jit(solution)/shard_map/reduce_scatter | solution.py:63
  456.4 22.1 %all-gather.14.cloned.1.call-done = bf16[1,1344,768]{2,1,0:T(8,128)(2,1)} async-done(((bf16[1,336,768]{2,1,0:T(8,128)(2,1)}), bf16[1,1344,768]{2,1,0:T(8,128)(2,1)}) %all-gather.14.cloned.1.call-update) | async-done | bytes 2064400 | tf_op jit(solution)/shard_map/all_gather | solution.py:51
  495.8 11.2 fusion.32
  511.7 44.2 %reduce-scatter.27.cloned.1.call-done = f32[1,336,768]{2,1,0:T(8,128)} async-done(((f32[1,1344,768]{2,1,0:T(8,128)}), f32[1,336,768]{2,1,0:T(8,128)}) %reduce-scatter.27.cloned.1.call-update) | async-done | bytes 1032208 | tf_op jit(solution)/shard_map/reduce_scatter | solution.py:55
  566.4 14.9 %all-gather.16.cloned.1.call-done = bf16[1,1344,768]{2,1,0:T(8,128)(2,1)} async-done(((bf16[1,336,768]{2,1,0:T(8,128)(2,1)}), bf16[1,1344,768]{2,1,0:T(8,128)(2,1)}) %all-gather.16.cloned.1.call-update) | async-done | bytes 2064400 | tf_op jit(solution)/shard_map/all_gather | solution.py:51
  581.2 13.0 fusion.7
  618.2 16.8 %reduce-scatter.33.cloned.1.call-done = f32[1,112,768]{2,1,0:T(8,128)} async-done(((f32[1,448,768]{2,1,0:T(8,128)}), f32[1,112,768]{2,1,0:T(8,128)}) %reduce-scatter.33.cloned.1.call-update) | async-done | bytes 344080 | tf_op jit(solution)/shard_map/reduce_scatter | solution.py:63
  638.7 43.6 %reduce-scatter.29.cloned.1.call-done = f32[1,336,768]{2,1,0:T(8,128)} async-done(((f32[1,1344,768]{2,1,0:T(8,128)}), f32[1,336,768]{2,1,0:T(8,128)}) %reduce-scatter.29.cloned.1.call-update) | async-done | bytes 1032208 | tf_op jit(solution)/shard_map/reduce_scatter | solution.py:63
  713.6 17.9 %multiply_reduce_fusion = (f32[3,1344]{1,0:T(4,128)S(1)}, f32[3,1344,1344]{1,2,0:T(8,128)}) fusion(f32[3,1344,1344]{1,2,0:T(8,128)} %copy-done, f32[3,1344]{1,0:T(4,128)S(1)} %log_add_fusion, bf16[1344,3,64]{0,2,1:T(8,128)(2,1)S(1)} %bitcast.437, bf16[1344,3,64]{0,2,1:T(8,128)(2,1)S(1)} %bitcast.433), kind=kOutput, calls=%fused_computation.1 | convolution fusion | flops 709886016 | bytes 44416512 | tf_op jit(solution)/shard_map/while/body/eval_jaxpr/rhe,she->hrs/dot_general | solution.py:105
  731.5 15.1 %multiply_convert_fusion = bf16[3,1344,1344]{1,2,0:T(8,128)(2,1)S(1)} fusion(f32[3,1344,1344]{1,2,0:T(8,128)} %get-tuple-element.247, f32[3,1344,1344]{1,2,0:T(8,128)} %copy-done, f32[3,1344]{1,0:T(4,128)S(1)} %get-tuple-element.246, f32[3,1344]{1,0:T(4,128)S(1)} %log_add_fusion), kind=kLoop, calls=%fused_computation | loop fusion | flops 21676032 | bytes 54222336 | tf_op jit(solution)/shard_map/while/body/eval_jaxpr/convert_element_type | solution.py:109
  757.4 11.1 convert_reduce_fusion.8
  813.2 39.0 %all-reduce.1 = (f32[3,2,192]{2,1,0:T(2,128)}, f32[5,768]{1,0:T(8,128)}, f32[2,768]{1,0:T(2,128)}) all-reduce(f32[3,2,192]{2,1,0:T(2,128)S(1)} %pad_maximum_fusion.4, f32[5,768]{1,0:T(8,128)S(1)} %concatenate.23, f32[2,768]{1,0:T(2,128)S(1)} %pad_maximum_fusion.5), channel_id=1, replica_groups=mesh['dp'=8,'mp'=4] {'dp'}, use_global_device_ids=true, to_apply=%region_66.67 | all-reduce | flops 6528 | bytes 52224 | tf_op jit(solution)/shard_map/psum | solution.py:428
  855.7 43.9 %all-reduce = (f32[5,768]{1,0:T(8,128)}, f32[5,768]{1,0:T(8,128)}) all-reduce(f32[5,768]{1,0:T(8,128)S(1)} %concatenate.18, f32[5,768]{1,0:T(8,128)S(1)} %concatenate.19), channel_id=1, replica_groups=mesh['dp'=8,'mp'=4] {'dp','mp'}, use_global_device_ids=true, to_apply=%region_52.53 | all-reduce | flops 7680 | bytes 61440 | tf_op jit(solution)/shard_map/psum | solution.py:431
  902.3 428.0 %all-reduce.5.cloned.1.call-done = (f32[3,3,768,192]{2,3,1,0:T(8,128)}, f32[3,192,768]{2,1,0:T(8,128)}, f32[2,768,768]{2,1,0:T(8,128)}, f32[2,768,768]{2,1,0:T(8,128)}) async-done(((f32[3,3,768,192]{2,3,1,0:T(8,128)}, f32[3,192,768]{2,1,0:T(8,128)}, f32[2,768,768]{2,1,0:T(8,128)}, f32[2,768,768]{2,1,0:T(8,128)}), (f32[3,3,768,192]{2,3,1,0:T(8,128)}, f32[3,192,768]{2,1,0:T(8,128)}, f32[2,768,768]{2,1,0:T(8,128)}, ...) | async-done | bytes 16515088 | tf_op jit(solution)/shard_map/psum | solution.py:428
  (584 shorter events, 325.6 us)
Async XLA Ops:
  7.2 32.7 %all-gather.8.cloned.1.call-start = ((), (), s32[]{:S(2)}) async-start(), calls=%async_computation.12 | async-start | bytes 2580480 | tf_op jit(solution)/shard_map/all_gather | solution.py:51
  11.9 147.1 %copy-start.103 = (f32[768]{0:T(1024)}, f32[768]{0:T(1024)S(1)}, u32[]{:S(2)}) copy-start(f32[768]{0:T(1024)S(1)} %get-tuple-element.268) | copy-start | bytes 9220
  11.9 221.4 %copy-start.109 = (f32[768]{0:T(1024)}, f32[768]{0:T(1024)S(1)}, u32[]{:S(2)}) copy-start(f32[768]{0:T(1024)S(1)} %get-tuple-element.269) | copy-start | bytes 9220
  12.0 285.9 %copy-start.111 = (f32[768]{0:T(1024)}, f32[768]{0:T(1024)S(1)}, u32[]{:S(2)}) copy-start(f32[768]{0:T(1024)S(1)} %get-tuple-element.270) | copy-start | bytes 9220
  14.6 100.5 %reduce-scatter.13.cloned.1.call-start = ((), (), s32[]{:S(2)}) async-start(), calls=%async_computation.13 | async-start | bytes 5160960 | tf_op jit(solution)/shard_map/reduce_scatter | solution.py:55
  70.9 71.0 %all-gather.10.cloned.1.call-start = ((), (), s32[]{:S(2)}) async-start(), calls=%async_computation.14 | async-start | bytes 2580480 | tf_op jit(solution)/shard_map/all_gather | solution.py:51
  72.2 129.9 %copy-start.101 = (f32[768]{0:T(1024)}, f32[768]{0:T(1024)S(1)}, u32[]{:S(2)}) copy-start(f32[768]{0:T(1024)S(1)} %get-tuple-element.188) | copy-start | bytes 9220
  119.3 82.7 %reduce-scatter.15.cloned.1.call-start = ((), (), s32[]{:S(2)}) async-start(), calls=%async_computation.15 | async-start | bytes 5160960 | tf_op jit(solution)/shard_map/reduce_scatter | solution.py:55
  157.7 74.2 %reduce-scatter.17.cloned.1.call-start = ((), (), s32[]{:S(2)}) async-start(), calls=%async_computation.16 | async-start | bytes 1720320 | tf_op jit(solution)/shard_map/reduce_scatter | solution.py:55
  176.7 79.8 %all-gather.12.cloned.1.call-start = ((), (), s32[]{:S(2)}) async-start(), calls=%async_computation.17 | async-start | bytes 2580480 | tf_op jit(solution)/shard_map/all_gather | solution.py:51
  204.3 92.1 %reduce-scatter.19.cloned.1.call-start = ((), (), s32[]{:S(2)}) async-start(), calls=%async_computation.18 | async-start | bytes 1720320 | tf_op jit(solution)/shard_map/reduce_scatter | solution.py:55
  269.2 77.3 %reduce-scatter.23.cloned.1.call-start = ((), (), s32[]{:S(2)}) async-start(), calls=%async_computation.20 | async-start | bytes 1720320 | tf_op jit(solution)/shard_map/reduce_scatter | solution.py:63
  319.0 57.8 %reduce-scatter.21.cloned.1.call-start = ((), (), s32[]{:S(2)}) async-start(), calls=%async_computation.19 | async-start | bytes 1720320 | tf_op jit(solution)/shard_map/reduce_scatter | solution.py:55
  322.1 131.0 %reduce-scatter.25.cloned.1.call-start = ((), (), s32[]{:S(2)}) async-start(), calls=%async_computation.21 | async-start | bytes 5160960 | tf_op jit(solution)/shard_map/reduce_scatter | solution.py:63
  408.5 70.0 %all-gather.14.cloned.1.call-start = ((), (), s32[]{:S(2)}) async-start(), calls=%async_computation.22 | async-start | bytes 2580480 | tf_op jit(solution)/shard_map/all_gather | solution.py:51
  456.0 99.9 %reduce-scatter.27.cloned.1.call-start = ((), (), s32[]{:S(2)}) async-start(), calls=%async_computation.23 | async-start | bytes 5160960 | tf_op jit(solution)/shard_map/reduce_scatter | solution.py:55
  511.6 69.6 %all-gather.16.cloned.1.call-start = ((), (), s32[]{:S(2)}) async-start(), calls=%async_computation.24 | async-start | bytes 2580480 | tf_op jit(solution)/shard_map/all_gather | solution.py:51
  558.6 46.4 %all-gather.18.cloned.1.call-start = ((), (), s32[]{:S(2)}) async-start(), calls=%async_computation.25 | async-start | bytes 2580480 | tf_op jit(solution)/shard_map/all_gather | solution.py:59
  559.6 75.4 %reduce-scatter.33.cloned.1.call-start = ((), (), s32[]{:S(2)}) async-start(), calls=%async_computation.29 | async-start | bytes 1720320 | tf_op jit(solution)/shard_map/reduce_scatter | solution.py:63
  566.1 116.2 %reduce-scatter.29.cloned.1.call-start = ((), (), s32[]{:S(2)}) async-start(), calls=%async_computation.26 | async-start | bytes 5160960 | tf_op jit(solution)/shard_map/reduce_scatter | solution.py:63
  618.1 93.0 %all-gather.20.cloned.1.call-start = ((), (), s32[]{:S(2)}) async-start(), calls=%async_computation.27 | async-start | bytes 2580480 | tf_op jit(solution)/shard_map/all_gather | solution.py:59
  688.6 118.6 %reduce-scatter.35.cloned.1.call-start = ((), (), s32[]{:S(2)}) async-start(), calls=%async_computation.30 | async-start | bytes 1720320 | tf_op jit(solution)/shard_map/reduce_scatter | solution.py:63
  709.0 143.2 %reduce-scatter.31.cloned.1.call-start = ((), (), s32[]{:S(2)}) async-start(), calls=%async_computation.28 | async-start | bytes 5160960 | tf_op jit(solution)/shard_map/reduce_scatter | solution.py:63
  773.9 556.3 %all-reduce.5.cloned.1.call-start = ((), (), s32[]{:S(2)}) async-start(), calls=%async_computation.31 | async-start | bytes 33030144 | tf_op jit(solution)/shard_map/psum | solution.py:428
  (164 other events, 2399.9 us)
Sparse Core Ops, SparseCore 0:
  14.7 25.0 all-gather.7
  71.0 44.0 reduce-scatter.12
  119.5 22.3 all-gather.9
  157.9 44.0 reduce-scatter.14
  205.0 26.9 reduce-scatter.16
  234.0 22.4 all-gather.11
  269.3 27.0 reduce-scatter.18
  319.1 27.3 reduce-scatter.22
  349.8 26.9 reduce-scatter.20
  408.6 44.4 reduce-scatter.24
  456.1 22.3 all-gather.13
  511.7 44.0 reduce-scatter.26
  558.8 22.3 all-gather.15
  582.6 22.3 all-gather.17
  608.0 26.9 reduce-scatter.32
  638.2 44.0 reduce-scatter.28
  688.7 22.3 all-gather.19
  713.5 26.9 reduce-scatter.34
  774.0 44.0 reduce-scatter.30
  823.9 506.2 all-reduce.4
where the time goes:
time: 1360 us; the launch traced here: 1350 us
  waiting for transfers between devices  852 us (63%)
  matrix products  211 us (16%)
  blocking collectives  130 us (10%)
  other arithmetic  90.1 us (7%)
  local copies, waits for them, and re-layouts  46 us (3%)
  between operations  17.5 us (1%)
    psum x1, waiting for transfers between devices, on_device(): lax.psum((merged[0], merged[1], merged[2], merged[3], merged[4], merged[5...  428 us
    reduce_scatter x6, waiting for transfers between devices, sum_rows(): lax.psum_scatter(partial_value, 'mp', scatter_dimension=1, tiled=True)  186 us
    reduce_scatter x6, waiting for transfers between devices, sum_grads(): lax.psum_scatter(partial_value, 'mp', scatter_dimension=1, tiled=True)  128 us
    all_gather x5, waiting for transfers between devices, gather_rows(): return lax.all_gather(normed, 'mp', axis=1, tiled=True)  97.5 us
    dot_general x20, matrix products, product(): jnp.einsum('crd,dh->crh', operand, weight, preferred_element_type=jnp.flo...  73.3 us
    unnamed x340, local copies, waits for them, and re-layouts  45.2 us
    dot_general x16, matrix products, product_back(): jnp.einsum('crh,dh->crd', gradient, weight, preferred_element_type=jnp.fl...  44.6 us
    psum x1, blocking collectives, on_device(): lax.psum((jnp.concatenate([enc_gains, dec_gains]), jnp.concatenate([enc_s...  43.9 us
  transfers between devices with their start and end apart: 20, of which 18 were waited for; matrix products, arithmetic and copies ran while one was open for 12% of the time, Pallas kernels for 0%

commit v1 on v0

--- a/solution.py
+++ b/solution.py
@@ -52,7 +52,9 @@
 
 
 def sum_rows(partial_value):
-    return lax.psum_scatter(partial_value, "mp", scatter_dimension=1, tiled=True)
+    return lax.psum_scatter(
+        partial_value.astype(jnp.bfloat16), "mp", scatter_dimension=1, tiled=True
+    ).astype(jnp.float32)
 
 
 def gather_grads(gradient):
@@ -60,7 +62,14 @@
 
 
 def sum_grads(partial_value):
-    return lax.psum_scatter(partial_value, "mp", scatter_dimension=1, tiled=True)
+    return lax.psum_scatter(
+        partial_value.astype(jnp.bfloat16), "mp", scatter_dimension=1, tiled=True
+    ).astype(jnp.float32)
+
+
+def sum_clips(values):
+    sent = tuple(value.astype(jnp.bfloat16) for value in values)
+    return tuple(value.astype(jnp.float32) for value in lax.psum(sent, "dp"))
 
 
 def score_block(queries, key_rows, causal):
@@ -411,23 +420,23 @@
         tokens, memory, dec_saved, dec_cot.astype(jnp.float32) * valid_rows, weights
     )
     encoded_grad = enc_cot.astype(jnp.float32) + memory_grad
-    frames_again, encoded_grad = lax.optimization_barrier((frames, encoded_grad))
-    unused, enc_saved = encoder_forward(frames_again, weights)
     frames_grad, enc_grads, enc_gains, enc_shifts = encoder_backward(
         frames, enc_saved, encoded_grad, weights
     )
+    dec_wide = sum_clips((dec_grads[0], dec_grads[2], dec_grads[4], dec_grads[6]))
+    enc_mlp = sum_clips((enc_grads[4], enc_grads[6]))
+    enc_attend = sum_clips((enc_grads[0], enc_grads[2]))
     merged = (
-        jnp.concatenate([enc_grads[0][None], dec_grads[0]]),
+        jnp.concatenate([enc_attend[0][None], dec_wide[0]]),
         jnp.concatenate([enc_grads[1][None], dec_grads[1]]),
-        jnp.concatenate([enc_grads[2][None], dec_grads[2]]),
+        jnp.concatenate([enc_attend[1][None], dec_wide[1]]),
         jnp.concatenate([enc_grads[3], dec_grads[3]]),
-        jnp.stack([enc_grads[4], dec_grads[4]]),
+        jnp.stack([enc_mlp[0], dec_wide[2]]),
         jnp.stack([enc_grads[5], dec_grads[5]]),
-        jnp.stack([enc_grads[6], dec_grads[6]]),
-    )
-    merged = lax.psum(
-        (merged[0], merged[1], merged[2], merged[3], merged[4], merged[5], merged[6]), "dp"
-    )
+        jnp.stack([enc_mlp[1], dec_wide[3]]),
+    )
+    narrow = lax.psum((merged[1], merged[3], merged[5]), "dp")
+    merged = (merged[0], narrow[0], merged[2], narrow[1], merged[4], narrow[2], merged[6])
     gain_grad, shift_grad = lax.psum(
         (jnp.concatenate([enc_gains, dec_gains]), jnp.concatenate([enc_shifts, dec_shifts])),
         ("dp", "mp"),

time: 1360 us -> 911 us (0.67)
  waiting for transfers between devices: 852 us -> 463 us
  matrix products: 211 us -> 180 us
  local copies, waits for them, and re-layouts: 46 us -> 20.9 us
    psum x1, waiting for transfers between devices: 428 us -> 190 us  [sum_clips(): return tuple((value.astype(jnp.float32) for value in lax.psum(sent, 'dp')))]
    reduce_scatter x12 -> x11, waiting for transfers between devices: 314 us -> 198 us  [the longest x5 106 us: sum_rows(): lax.psum_scatter(partial_value.astype(jnp.bfloat16), 'mp', scatter_dimens...]
    all_gather x5 -> x3, waiting for transfers between devices: 97.5 us -> 58.2 us  [gather_rows(): return lax.all_gather(normed, 'mp', axis=1, tiled=True)]
    dot_general x20 -> x16, matrix products: 73.3 us -> 46.9 us  [product(): jnp.einsum('crd,dh->crh', operand, weight, preferred_element_type=jnp.flo...]
    unnamed x340 -> x330, local copies, waits for them, and re-layouts: 45.2 us -> 20.2 us
  transfers between devices with their start and end apart: 20 -> 17, of which waited for: 18 -> 15; matrix products, arithmetic and copies ran while one was open for 12% -> 17% of each run, Pallas kernels for 0% -> 0%
where the time goes in v1:
time: 911 us; the launch traced here: 901 us
  waiting for transfers between devices  463 us (51%)
  matrix products  180 us (20%)
  blocking collectives  129 us (14%)
  other arithmetic  88.3 us (10%)
  local copies, waits for them, and re-layouts  20.9 us (2%)
  between operations  17.3 us (2%)
    psum x1, waiting for transfers between devices, sum_clips(): return tuple((value.astype(jnp.float32) for value in lax.psum(sent, 'dp')))  190 us
    reduce_scatter x5, waiting for transfers between devices, sum_rows(): lax.psum_scatter(partial_value.astype(jnp.bfloat16), 'mp', scatter_dimens...  106 us
    reduce_scatter x6, waiting for transfers between devices, sum_grads(): lax.psum_scatter(partial_value.astype(jnp.bfloat16), 'mp', scatter_dimens...  92.7 us
    all_gather x3, waiting for transfers between devices, gather_rows(): return lax.all_gather(normed, 'mp', axis=1, tiled=True)  58.2 us
    dot_general x16, matrix products, product(): jnp.einsum('crd,dh->crh', operand, weight, preferred_element_type=jnp.flo...  46.9 us
    dot_general x16, matrix products, product_back(): jnp.einsum('crh,dh->crd', gradient, weight, preferred_element_type=jnp.fl...  45.1 us
    psum x1, blocking collectives, on_device(): lax.psum((jnp.concatenate([enc_gains, dec_gains]), jnp.concatenate([enc_s...  41.8 us
    psum x1, blocking collectives, on_device(): narrow = lax.psum((merged[1], merged[3], merged[5]), 'dp')  40.1 us
  transfers between devices with their start and end apart: 17, of which 15 were waited for; matrix products, arithmetic and copies ran while one was open for 17% of the time, Pallas kernels for 0%

profile of v1, /device:TPU:0, one launch (start us, length us, event | category | flops | bytes accessed | tf_op | source)
XLA Modules:
  0.0 901.2 jit_solution(270581584059114808)
XLA Ops:
  14.7 25.2 %all-gather.6.cloned.1.call-done = bf16[1,1344,768]{2,1,0:T(8,128)(2,1)} async-done(((bf16[1,336,768]{2,1,0:T(8,128)(2,1)}), bf16[1,1344,768]{2,1,0:T(8,128)(2,1)}) %all-gather.6.cloned.1.call-update) | async-done | bytes 2064400 | tf_op jit(solution)/shard_map/all_gather | solution.py:51
  57.2 11.3 %fusion.23 = bf16[3,64,1344]{2,1,0:T(8,128)(2,1)S(1)} fusion(bf16[1344,3,64]{0,2,1:T(8,128)(2,1)S(1)} %bitcast.413, f32[3,1344,1344]{1,2,0:T(8,128)} %copy-done, f32[3,1344]{1,0:T(4,128)S(1)} %log_add_fusion), kind=kOutput, calls=%fused_computation.68 | convolution fusion | flops 704729088 | bytes 22724352 | tf_op jit(solution)/shard_map/while/body/eval_jaxpr/hrs,she->rhe/dot_general | solution.py:98
  72.1 30.7 %reduce-scatter.12.cloned.1.call-done = bf16[1,336,768]{2,1,0:T(8,128)(2,1)} async-done(((bf16[1,1344,768]{2,1,0:T(8,128)(2,1)}), bf16[1,336,768]{2,1,0:T(8,128)(2,1)}) %reduce-scatter.12.cloned.1.call-update) | async-done | bytes 516112 | tf_op jit(solution)/shard_map/reduce_scatter | solution.py:55
  107.2 22.0 %all-gather.8.cloned.1.call-done = bf16[1,1344,768]{2,1,0:T(8,128)(2,1)} async-done(((bf16[1,336,768]{2,1,0:T(8,128)(2,1)}), bf16[1,1344,768]{2,1,0:T(8,128)(2,1)}) %all-gather.8.cloned.1.call-update) | async-done | bytes 2064400 | tf_op jit(solution)/shard_map/all_gather | solution.py:51
  129.2 13.5 %multiply_convert_fusion.2 = (bf16[1344,768]{1,0:T(8,128)(2,1)S(1)}, f32[1344,768]{1,0:T(8,128)}, f32[1344,768]{1,0:T(8,128)}) fusion(f32[768]{0:T(1024)S(1)} %get-tuple-element.183, bf16[2,768,768]{2,1,0:T(8,128)(2,1)} %param.23, bf16[1,1344,768]{2,1,0:T(8,128)(2,1)} %all-gather.8.cloned.1.call-done), kind=kOutput, calls=%fused_computation.20 | convolution fusion | flops 1653571584 | bytes 13569024 | tf_op jit(solution)/shard_map/crd,dh->crh/dot_general | solution.py:35
  148.3 8.1 all_gather.35
  163.9 14.6 %reduce-scatter.14.cloned.1.call-done = bf16[1,336,768]{2,1,0:T(8,128)(2,1)} async-done(((bf16[1,1344,768]{2,1,0:T(8,128)(2,1)}), bf16[1,336,768]{2,1,0:T(8,128)(2,1)}) %reduce-scatter.14.cloned.1.call-update) | async-done | bytes 516112 | tf_op jit(solution)/shard_map/reduce_scatter | solution.py:55
  180.7 23.5 %reduce-scatter.16.cloned.1.call-done = bf16[1,112,768]{2,1,0:T(8,128)(2,1)} async-done(((bf16[1,448,768]{2,1,0:T(8,128)(2,1)}), bf16[1,112,768]{2,1,0:T(8,128)(2,1)}) %reduce-scatter.16.cloned.1.call-update) | async-done | bytes 172048 | tf_op jit(solution)/shard_map/reduce_scatter | solution.py:55
  217.6 11.1 %all-gather.10.cloned.1.call-done = bf16[1,1344,768]{2,1,0:T(8,128)(2,1)} async-done(((bf16[1,336,768]{2,1,0:T(8,128)(2,1)}), bf16[1,1344,768]{2,1,0:T(8,128)(2,1)}) %all-gather.10.cloned.1.call-update) | async-done | bytes 2064400 | tf_op jit(solution)/shard_map/all_gather | solution.py:51
  241.3 8.1 all_gather.39
  249.4 14.0 %reduce-scatter.18.cloned.1.call-done = bf16[1,112,768]{2,1,0:T(8,128)(2,1)} async-done(((bf16[1,448,768]{2,1,0:T(8,128)(2,1)}), bf16[1,112,768]{2,1,0:T(8,128)(2,1)}) %reduce-scatter.18.cloned.1.call-update) | async-done | bytes 172048 | tf_op jit(solution)/shard_map/reduce_scatter | solution.py:55
  286.5 19.7 %reduce-scatter.22.cloned.1.call-done = bf16[1,112,768]{2,1,0:T(8,128)(2,1)} async-done(((bf16[1,448,768]{2,1,0:T(8,128)(2,1)}), bf16[1,112,768]{2,1,0:T(8,128)(2,1)}) %reduce-scatter.22.cloned.1.call-update) | async-done | bytes 172048 | tf_op jit(solution)/shard_map/reduce_scatter | solution.py:65
  309.1 22.9 %reduce-scatter.20.cloned.1.call-done = bf16[1,112,768]{2,1,0:T(8,128)(2,1)} async-done(((bf16[1,448,768]{2,1,0:T(8,128)(2,1)}), bf16[1,112,768]{2,1,0:T(8,128)(2,1)}) %reduce-scatter.20.cloned.1.call-update) | async-done | bytes 172048 | tf_op jit(solution)/shard_map/reduce_scatter | solution.py:55
  362.5 31.7 %reduce-scatter.24.cloned.1.call-done = bf16[1,336,768]{2,1,0:T(8,128)(2,1)} async-done(((bf16[1,1344,768]{2,1,0:T(8,128)(2,1)}), bf16[1,336,768]{2,1,0:T(8,128)(2,1)}) %reduce-scatter.24.cloned.1.call-update) | async-done | bytes 516112 | tf_op jit(solution)/shard_map/reduce_scatter | solution.py:65
  403.1 15.8 %all-gather.12.cloned.1.call-done = bf16[1,1344,768]{2,1,0:T(8,128)(2,1)} async-done(((bf16[1,336,768]{2,1,0:T(8,128)(2,1)}), bf16[1,1344,768]{2,1,0:T(8,128)(2,1)}) %all-gather.12.cloned.1.call-update) | async-done | bytes 2064400 | tf_op jit(solution)/shard_map/all_gather | solution.py:61
  418.8 7.9 convert_reduce_fusion
  434.5 10.1 %reduce-scatter.30.cloned.1.call-done = bf16[1,112,768]{2,1,0:T(8,128)(2,1)} async-done(((bf16[1,448,768]{2,1,0:T(8,128)(2,1)}), bf16[1,112,768]{2,1,0:T(8,128)(2,1)}) %reduce-scatter.30.cloned.1.call-update) | async-done | bytes 172048 | tf_op jit(solution)/shard_map/reduce_scatter | solution.py:65
  448.1 31.1 %reduce-scatter.26.cloned.1.call-done = bf16[1,336,768]{2,1,0:T(8,128)(2,1)} async-done(((bf16[1,1344,768]{2,1,0:T(8,128)(2,1)}), bf16[1,336,768]{2,1,0:T(8,128)(2,1)}) %reduce-scatter.26.cloned.1.call-update) | async-done | bytes 516112 | tf_op jit(solution)/shard_map/reduce_scatter | solution.py:65
  510.3 17.6 %multiply_reduce_fusion = (f32[3,1344]{1,0:T(4,128)S(1)}, f32[3,1344,1344]{1,2,0:T(8,128)}) fusion(f32[3,1344,1344]{1,2,0:T(8,128)} %copy-done, f32[3,1344]{1,0:T(4,128)S(1)} %copy-done.56, bf16[1344,3,64]{0,2,1:T(8,128)(2,1)S(1)} %bitcast.417, bf16[1344,3,64]{0,2,1:T(8,128)(2,1)S(1)} %bitcast.414), kind=kOutput, calls=%fused_computation.1 | convolution fusion | flops 709886016 | bytes 44416512 | tf_op jit(solution)/shard_map/while/body/eval_jaxpr/rhe,she->hrs/dot_general | solution.py:114
  527.9 15.1 %multiply_convert_fusion = bf16[3,1344,1344]{1,2,0:T(8,128)(2,1)S(1)} fusion(f32[3,1344,1344]{1,2,0:T(8,128)} %get-tuple-element.225, f32[3,1344,1344]{1,2,0:T(8,128)} %copy-done, f32[3,1344]{1,0:T(4,128)S(1)} %get-tuple-element.224, f32[3,1344]{1,0:T(4,128)S(1)} %copy-done.56), kind=kLoop, calls=%fused_computation | loop fusion | flops 21676032 | bytes 54222336 | tf_op jit(solution)/shard_map/while/body/eval_jaxpr/convert_element_type | solution.py:118
  555.8 11.6 %convert_reduce_fusion.11 = (f32[3,64]{1,0:T(4,128)}, bf16[3,64,1344]{2,1,0:T(8,128)(2,1)S(1)}) fusion(bf16[1344,3,64]{0,2,1:T(8,128)(2,1)S(1)} %bitcast.418, f32[3,1344,1344]{1,2,0:T(8,128)} %copy-done, f32[3,1344]{1,0:T(4,128)S(1)} %copy-done.56), kind=kOutput, calls=%fused_computation.214 | convolution fusion | flops 705244992 | bytes 22725120 | tf_op jit(solution)/shard_map/while/body/eval_jaxpr/hrs,rhe->she/dot_general | solution.py:128
  606.2 40.1 %all-reduce.1 = (f32[3,2,192]{2,1,0:T(2,128)}, f32[5,768]{1,0:T(8,128)}, f32[2,768]{1,0:T(2,128)}) all-reduce(f32[3,2,192]{2,1,0:T(2,128)S(1)} %pad_maximum_fusion.2, f32[5,768]{1,0:T(8,128)S(1)} %concatenate.31, f32[2,768]{1,0:T(2,128)S(1)} %pad_maximum_fusion.3), channel_id=1, replica_groups=mesh['dp'=8,'mp'=4] {'dp'}, use_global_device_ids=true, to_apply=%region_60.61 | all-reduce | flops 6528 | bytes 52224 | tf_op jit(solution)/shard_map/psum | solution.py:438
  649.7 41.8 %all-reduce = (f32[5,768]{1,0:T(8,128)}, f32[5,768]{1,0:T(8,128)}) all-reduce(f32[5,768]{1,0:T(8,128)S(1)} %concatenate.24, f32[5,768]{1,0:T(8,128)S(1)} %concatenate.25), channel_id=1, replica_groups=mesh['dp'=8,'mp'=4] {'dp','mp'}, use_global_device_ids=true, to_apply=%region_45.46 | all-reduce | flops 7680 | bytes 61440 | tf_op jit(solution)/shard_map/psum | solution.py:440
  693.4 190.4 %all-reduce.5.cloned.1.call-done = (bf16[2,3,768,192]{2,3,1,0:T(8,128)(2,1)}, bf16[1,3,768,192]{2,3,1,0:T(8,128)(2,1)}, bf16[2,192,768]{2,1,0:T(8,128)(2,1)}, bf...) async-done(((bf16[2,3,768,192]{2,3,1,0:T(8,128)(2,1)}, ...) | async-done | bytes 8257552 | tf_op jit(solution)/shard_map/psum | solution.py:72
  (546 shorter events, 246.3 us)
Async XLA Ops:
  7.2 32.7 %all-gather.6.cloned.1.call-start = ((), (), s32[]{:S(2)}) async-start(), calls=%async_computation.11 | async-start | bytes 2580480 | tf_op jit(solution)/shard_map/all_gather | solution.py:51
  11.9 93.6 %copy-start.97 = (f32[768]{0:T(1024)}, f32[768]{0:T(1024)S(1)}, u32[]{:S(2)}) copy-start(f32[768]{0:T(1024)S(1)} %get-tuple-element.245) | copy-start | bytes 9220
  11.9 136.3 %copy-start.101 = (f32[768]{0:T(1024)}, f32[768]{0:T(1024)S(1)}, u32[]{:S(2)}) copy-start(f32[768]{0:T(1024)S(1)} %get-tuple-element.246) | copy-start | bytes 9220
  11.9 194.6 %copy-start.103 = (f32[768]{0:T(1024)}, f32[768]{0:T(1024)S(1)}, u32[]{:S(2)}) copy-start(f32[768]{0:T(1024)S(1)} %get-tuple-element.247) | copy-start | bytes 9220
  11.9 252.8 %copy-start.109 = (f32[768]{0:T(1024)}, f32[768]{0:T(1024)S(1)}, u32[]{:S(2)}) copy-start(f32[768]{0:T(1024)S(1)} %get-tuple-element.248) | copy-start | bytes 9220
  14.6 88.2 %reduce-scatter.12.cloned.1.call-start = ((), (), s32[]{:S(2)}) async-start(), calls=%async_computation.12 | async-start | bytes 2580480 | tf_op jit(solution)/shard_map/reduce_scatter | solution.py:55
  71.4 57.8 %all-gather.8.cloned.1.call-start = ((), (), s32[]{:S(2)}) async-start(), calls=%async_computation.13 | async-start | bytes 2580480 | tf_op jit(solution)/shard_map/all_gather | solution.py:51
  106.7 71.9 %reduce-scatter.14.cloned.1.call-start = ((), (), s32[]{:S(2)}) async-start(), calls=%async_computation.14 | async-start | bytes 2580480 | tf_op jit(solution)/shard_map/reduce_scatter | solution.py:55
  147.2 57.0 %reduce-scatter.16.cloned.1.call-start = ((), (), s32[]{:S(2)}) async-start(), calls=%async_computation.15 | async-start | bytes 860160 | tf_op jit(solution)/shard_map/reduce_scatter | solution.py:55
  163.9 64.8 %all-gather.10.cloned.1.call-start = ((), (), s32[]{:S(2)}) async-start(), calls=%async_computation.16 | async-start | bytes 2580480 | tf_op jit(solution)/shard_map/all_gather | solution.py:51
  180.7 82.7 %reduce-scatter.18.cloned.1.call-start = ((), (), s32[]{:S(2)}) async-start(), calls=%async_computation.17 | async-start | bytes 860160 | tf_op jit(solution)/shard_map/reduce_scatter | solution.py:55
  240.4 65.7 %reduce-scatter.22.cloned.1.call-start = ((), (), s32[]{:S(2)}) async-start(), calls=%async_computation.19 | async-start | bytes 860160 | tf_op jit(solution)/shard_map/reduce_scatter | solution.py:65
  283.0 49.0 %reduce-scatter.20.cloned.1.call-start = ((), (), s32[]{:S(2)}) async-start(), calls=%async_computation.18 | async-start | bytes 860160 | tf_op jit(solution)/shard_map/reduce_scatter | solution.py:55
  286.5 107.8 %reduce-scatter.24.cloned.1.call-start = ((), (), s32[]{:S(2)}) async-start(), calls=%async_computation.20 | async-start | bytes 2580480 | tf_op jit(solution)/shard_map/reduce_scatter | solution.py:65
  362.5 56.4 %all-gather.12.cloned.1.call-start = ((), (), s32[]{:S(2)}) async-start(), calls=%async_computation.21 | async-start | bytes 2580480 | tf_op jit(solution)/shard_map/all_gather | solution.py:61
  396.3 48.4 %reduce-scatter.30.cloned.1.call-start = ((), (), s32[]{:S(2)}) async-start(), calls=%async_computation.25 | async-start | bytes 860160 | tf_op jit(solution)/shard_map/reduce_scatter | solution.py:65
  402.6 76.6 %reduce-scatter.26.cloned.1.call-start = ((), (), s32[]{:S(2)}) async-start(), calls=%async_computation.22 | async-start | bytes 2580480 | tf_op jit(solution)/shard_map/reduce_scatter | solution.py:65
  431.3 76.5 %all-gather.14.cloned.1.call-start = ((), (), s32[]{:S(2)}) async-start(), calls=%async_computation.23 | async-start | bytes 2580480 | tf_op jit(solution)/shard_map/all_gather | solution.py:61
  485.3 112.2 %reduce-scatter.32.cloned.1.call-start = ((), (), s32[]{:S(2)}) async-start(), calls=%async_computation.26 | async-start | bytes 860160 | tf_op jit(solution)/shard_map/reduce_scatter | solution.py:65
  507.0 139.3 %reduce-scatter.28.cloned.1.call-start = ((), (), s32[]{:S(2)}) async-start(), calls=%async_computation.24 | async-start | bytes 2580480 | tf_op jit(solution)/shard_map/reduce_scatter | solution.py:65
  573.2 310.6 %all-reduce.5.cloned.1.call-start = ((), (), s32[]{:S(2)}) async-start(), calls=%async_computation.27 | async-start | bytes 16515072 | tf_op jit(solution)/shard_map/psum | solution.py:72
  603.8 87.7 %copy-start.9 = (bf16[1,336,768]{2,1,0:T(8,128)(2,1)S(1)}, bf16[1,336,768]{2,1,0:T(8,128)(2,1)}, u32[]{:S(2)}) copy-start(bf16[1,336,768]{2,1,0:T(8,128)(2,1)} %reduce-scatter.12.cloned.1.call-done) | copy-start | bytes 1548292
  603.8 87.7 %copy-start.21 = (bf16[1,336,768]{2,1,0:T(8,128)(2,1)S(1)}, bf16[1,336,768]{2,1,0:T(8,128)(2,1)}, u32[]{:S(2)}) copy-start(bf16[1,336,768]{2,1,0:T(8,128)(2,1)} %reduce-scatter.26.cloned.1.call-done) | copy-start | bytes 1548292
  603.8 87.7 %copy-start.42 = (bf16[1,336,768]{2,1,0:T(8,128)(2,1)S(1)}, bf16[1,336,768]{2,1,0:T(8,128)(2,1)}, u32[]{:S(2)}) copy-start(bf16[1,336,768]{2,1,0:T(8,128)(2,1)} %param.26) | copy-start | bytes 1548292
  (158 other events, 1848.9 us)
Sparse Core Ops, SparseCore 0:
  14.7 25.0 all-gather.5
  71.5 31.1 reduce-scatter.11
  106.8 22.3 all-gather.7
  147.3 31.1 reduce-scatter.13
  181.5 22.6 reduce-scatter.15
  206.2 22.3 all-gather.9
  240.6 22.7 reduce-scatter.17
  283.1 23.0 reduce-scatter.21
  309.3 22.6 reduce-scatter.19
  362.6 31.6 reduce-scatter.23
  396.4 22.3 all-gather.11
  422.0 22.6 reduce-scatter.29
  448.0 31.1 reduce-scatter.25
  485.4 22.3 all-gather.13
  510.2 22.6 reduce-scatter.31
  573.3 31.2 reduce-scatter.27
  611.2 272.5 all-reduce.4

commit v2 on v1

--- a/solution.py
+++ b/solution.py
@@ -1,13 +1,475 @@
+import functools
+import math
+
 import jax
 import jax.numpy as jnp
 from jax import lax
+from jax.experimental import pallas as pl
+from jax.experimental.pallas import tpu as pltpu
 from jax.sharding import PartitionSpec as P
 
 HEAD = 64
-
-
 epsilon = 1e-05
 masked_score = -1e30
+f32 = jnp.float32
+bf16 = jnp.bfloat16
+NN = (((1,), (0,)), ((), ()))
+NT = (((1,), (1,)), ((), ()))
+TN = (((0,), (0,)), ((), ()))
+SCALE = HEAD ** (-0.5)
+SCORE_TO_LOG2 = SCALE * math.log2(math.e)
+ANY = pl.BlockSpec(memory_space=pl.ANY)
+VMEM = pl.BlockSpec(memory_space=pltpu.VMEM)
+
+
+def dot(a, b, dims=NN):
+    return lax.dot_general(a, b, dims, preferred_element_type=f32)
+
+
+def window(start, size):
+    return pl.ds(pl.multiple_of(start, 16), size)
+
+
+def places():
+    me = lax.axis_index("mp")
+    core = lax.rem(me, 2)
+    mate = me + 1 - 2 * core
+    opp = lax.rem(me + 2, 4)
+    diag = lax.rem(mate + 2, 4)
+    return me, mate, opp, diag
+
+
+def remote(src, dst, sent, landed, axis, index):
+    return pltpu.make_async_remote_copy(
+        src_ref=src,
+        dst_ref=dst,
+        send_sem=sent,
+        recv_sem=landed,
+        device_id={axis: index},
+        device_id_type=pl.DeviceIdType.MESH,
+    )
+
+
+class Gather:
+    def __init__(self, buf, sems, rows, step):
+        self.buf, self.sems, self.rows, self.step = buf, sems, rows, step
+        self.me, self.mate_id, self.opp_id, self.diag_id = places()
+
+    def at(self, block, j):
+        return window(block * self.rows + j * self.step, self.step)
+
+    def copy(self, kind, block, j, target):
+        part = self.buf.at[self.at(block, j)]
+        return remote(part, part, self.sems.at[2 * kind, j], self.sems.at[2 * kind + 1, j], "mp", target)
+
+    def send(self, j):
+        self.copy(0, self.me, j, self.opp_id).start()
+        self.copy(1, self.me, j, self.mate_id).start()
+
+    def mate(self, j):
+        self.copy(1, self.mate_id, j, self.mate_id).wait_recv()
+
+    def opp(self, j):
+        self.copy(0, self.opp_id, j, self.opp_id).wait_recv()
+        self.copy(2, self.opp_id, j, self.mate_id).start()
+
+    def diag(self, j):
+        self.copy(2, self.diag_id, j, self.mate_id).wait_recv()
+
+    def close(self, j):
+        self.copy(0, self.me, j, self.opp_id).wait_send()
+        self.copy(1, self.me, j, self.mate_id).wait_send()
+        self.copy(2, self.opp_id, j, self.mate_id).wait_send()
+
+
+class Scatter:
+    def __init__(self, own, send, land, ysend, yland, sems, rows, step):
+        self.own, self.out, self.land, self.ysend, self.yland = own, send, land, ysend, yland
+        self.sems, self.rows, self.step = sems, rows, step
+        self.me, self.mate_id, self.opp_id, self.diag_id = places()
+
+    def near(self, half, j):
+        part = window(half * self.rows + j * self.step, self.step)
+        return remote(
+            self.out.at[part], self.land.at[part],
+            self.sems.at[2 * half, j], self.sems.at[2 * half + 1, j], "mp", self.mate_id,
+        )
+
+    def far(self, j):
+        part = window(j * self.step, self.step)
+        return remote(
+            self.ysend.at[part], self.yland.at[part],
+            self.sems.at[4, j], self.sems.at[5, j], "mp", self.opp_id,
+        )
+
+    def put_diag(self, j, value):
+        self.out[window(j * self.step, self.step), :] = value.astype(bf16)
+        self.near(0, j).start()
+
+    def put_opp(self, j, value):
+        part = window(j * self.step, self.step)
+        self.near(0, j).wait_recv()
+        self.ysend[part, :] = (value + self.land[part, :].astype(f32)).astype(bf16)
+        self.far(j).start()
+
+    def put_mate(self, j, value):
+        self.out[window(self.rows + j * self.step, self.step), :] = value.astype(bf16)
+        self.near(1, j).start()
+
+    def put_own(self, j, value):
+        self.own[window(j * self.step, self.step), :] = value
+
+    def total(self, j):
+        self.near(1, j).wait_recv()
+        self.far(j).wait_recv()
+        part = window(j * self.step, self.step)
+        near = self.land[window(self.rows + j * self.step, self.step), :].astype(f32)
+        return self.own[part, :] + near + self.yland[part, :].astype(f32)
+
+    def close(self, j):
+        self.near(0, j).wait_send()
+        self.near(1, j).wait_send()
+        self.far(j).wait_send()
+
+
+def scatter_shapes(rows, width, steps):
+    return [
+        pltpu.VMEM((rows, width), f32),
+        pltpu.VMEM((2 * rows, width), bf16),
+        pltpu.VMEM((2 * rows, width), bf16),
+        pltpu.VMEM((rows, width), bf16),
+        pltpu.VMEM((rows, width), bf16),
+        pltpu.SemaphoreType.DMA((6, steps)),
+    ]
+
+
+def meet(partners):
+    barrier = pltpu.get_barrier_semaphore()
+    for axis, index in partners:
+        pl.semaphore_signal(barrier, inc=1, device_id={axis: index}, device_id_type=pl.DeviceIdType.MESH)
+    pl.semaphore_wait(barrier, len(partners))
+
+
+def layer_norm(rows_in, gain_row, shift_row):
+    average = jnp.mean(rows_in, axis=-1, keepdims=True)
+    centred = rows_in - average
+    spread = jnp.mean(centred * centred, axis=-1, keepdims=True)
+    return centred * lax.rsqrt(spread + epsilon) * gain_row + shift_row
+
+
+def head_row(width, h):
+    lane = lax.broadcasted_iota(jnp.int32, (1, width), 1)
+    return jnp.where((lane >= h * HEAD) & (lane < (h + 1) * HEAD), 1.0, 0.0).astype(f32)
+
+
+def attend_rows(q_ref, k_ref, v_ref, out_ref, log_ref, start, size, causal):
+    width = q_ref.shape[1]
+    part = window(start, size)
+    queries = q_ref[part, :]
+    keys = k_ref[...]
+    values = v_ref[...]
+    lane = lax.broadcasted_iota(jnp.int32, (size, log_ref.shape[1]), 1)
+    mixed = jnp.zeros((size, width), f32)
+    logs = jnp.zeros((size, log_ref.shape[1]), f32)
+    for h in range(width // HEAD):
+        picked = head_row(width, h)
+        scores = dot(queries * picked.astype(bf16), keys, NT)
+        if causal:
+            row_index = lax.broadcasted_iota(jnp.int32, scores.shape, 0) + start
+            col_index = lax.broadcasted_iota(jnp.int32, scores.shape, 1)
+            scores = jnp.where(col_index <= row_index, scores, masked_score)
+        highest = jnp.max(scores, axis=-1, keepdims=True)
+        powers = jnp.exp2((scores - highest) * SCORE_TO_LOG2)
+        total = jnp.sum(powers, axis=-1, keepdims=True)
+        mixed = mixed + dot(powers.astype(bf16), values) * (picked / total)
+        logs = jnp.where(lane == h, highest * SCORE_TO_LOG2 + jnp.log2(total), logs)
+    out_ref[part, :] = mixed.astype(bf16)
+    log_ref[part, :] = logs
+
+
+def gelu_parts(hidden):
+    below = 0.5 + 0.5 * lax.erf(hidden * (0.5 ** 0.5))
+    density = jnp.exp2(hidden * hidden * (-0.5 * math.log2(math.e))) * ((2 * math.pi) ** (-0.5))
+    return hidden * below, below + hidden * density
+
+
+def forward_kernel(
+    R, T,
+    enc_in, dec_in, gain_ref, shift_ref, qv_bias, out_bias, fc1_bias, qkv, proj, fc1, fc2,
+    o_enc, o_g1, o_q, o_k, o_v, o_a, o_l, o_mid, o_g2, o_e, o_gd, o_g3, o_ck, o_cv,
+    o_m1, o_sq, o_sk, o_sv, o_sa, o_sl, o_as, o_m2, o_cq,
+    w_e, w_s, w_c, w_pe, w_ps, w_f1, w_f2,
+    g1, q, k, v, a, l, lt, mid, g2, e, gd, g3, ck, cv, m1, sq, sk, sv, sa, sl, slt, after, m2, cq, enc,
+    *rest,
+):
+    rest = list(rest)
+    take = lambda n: [rest.pop(0) for _ in range(n)]
+    rs1, rs2, rsd = take(6), take(6), take(6)
+    ag1, ag2, ag3, agd1, agd2 = take(5)
+    load_sem, save_sem = take(2)
+    S = T
+    steps = R // S
+    me, mate, opp, diag = places()
+    loads = [
+        pltpu.make_async_copy(src, dst, load_sem.at[i])
+        for i, (src, dst) in enumerate(
+            [(qkv.at[0], w_e), (qkv.at[1], w_s), (qkv.at[2], w_c), (proj.at[0], w_pe), (proj.at[1], w_ps),
+             (fc1.at[0], w_f1), (fc2.at[0], w_f2)]
+        )
+    ]
+    for load in loads:
+        load.start()
+    saves = []
+
+    def save(src, dst):
+        copy = pltpu.make_async_copy(src, dst, save_sem.at[len(saves)])
+        copy.start()
+        saves.append(copy)
+
+    gains = gain_ref[...].astype(f32)
+    shifts = shift_ref[...].astype(f32)
+    branch_bias = out_bias[...].astype(f32)
+    head_bias = qv_bias[...].astype(f32)
+    wide_bias = fc1_bias[...].astype(f32)
+
+    meet([("mp", mate), ("mp", opp)])
+
+    gd1 = Gather(m1, agd1, T, S)
+    m1[window(me * T, T), :] = layer_norm(dec_in[0].astype(f32), gains[2:3], shifts[2:3]).astype(bf16)
+    gd1.send(0)
+    ge1 = Gather(g1, ag1, R, S)
+
+    @pl.loop(0, steps)
+    def _(j):
+        rows = enc_in[0, window(j * S, S), :].astype(f32)
+        g1[window(me * R + j * S, S), :] = layer_norm(rows, gains[0:1], shifts[0:1]).astype(bf16)
+        ge1.send(j)
+
+    def project_block(block):
+        part = window(block * R, R)
+        rows = g1[part, :]
+        q[part, :] = (dot(rows, w_e[0]) + head_bias[0, 0:1]).astype(bf16)
+        k[part, :] = dot(rows, w_e[1]).astype(bf16)
+        v[part, :] = (dot(rows, w_e[2]) + head_bias[0, 1:2]).astype(bf16)
+
+    loads[0].wait()
+
+    @pl.loop(0, steps)
+    def _(j):
+        ge1.mate(j)
+
+    @pl.loop(0, 2)
+    def _(i):
+        project_block(me + i * (mate - me))
+
+    gd1.mate(0)
+    gd1.opp(0)
+    gd1.diag(0)
+    save(m1, o_m1)
+    loads[1].wait()
+    sq[...] = (dot(m1[...], w_s[0]) + head_bias[1, 0:1]).astype(bf16)
+    sk[...] = dot(m1[...], w_s[1]).astype(bf16)
+    sv[...] = (dot(m1[...], w_s[2]) + head_bias[1, 1:2]).astype(bf16)
+    save(sq, o_sq)
+    save(sk, o_sk)
+    save(sv, o_sv)
+
+    @pl.loop(0, 2)
+    def _(i):
+        attend_rows(sq, sk, sv, sa, sl, i * 2 * T, 2 * T, True)
+
+    save(sa, o_sa)
+    slt[...] = jnp.transpose(sl[...])[0:8]
+    save(slt, o_sl)
+    loads[4].wait()
+    sd = Scatter(*rsd, T, S)
+    sd.put_diag(0, dot(sa[window(diag * T, T), :], w_ps[...]))
+    sd.put_opp(0, dot(sa[window(opp * T, T), :], w_ps[...]))
+    sd.put_mate(0, dot(sa[window(mate * T, T), :], w_ps[...]))
+    sd.put_own(0, dot(sa[window(me * T, T), :], w_ps[...]))
+
+    @pl.loop(0, steps)
+    def _(j):
+        ge1.opp(j)
+
+    @pl.loop(0, steps)
+    def _(j):
+        ge1.diag(j)
+
+    @pl.loop(0, 2)
+    def _(i):
+        project_block(opp + i * (diag - opp))
+
+    save(g1, o_g1)
+    save(q, o_q)
+    save(k, o_k)
+    save(v, o_v)
+    loads[3].wait()
+    s1 = Scatter(*rs1, R, S)
+
+    def attend_block(block, put):
+        attend_rows(q, k, v, a, l, block * R, R, False)
+
+        @pl.loop(0, steps)
+        def _(j):
+            put(j, dot(a[window(block * R + j * S, S), :], w_pe[...]))
+
+    attend_block(diag, s1.put_diag)
+    attend_block(opp, s1.put_opp)
+
+    after[...] = dec_in[0].astype(f32) + sd.total(0) + branch_bias[2:3]
+    gd2 = Gather(m2, agd2, T, S)
+    m2[window(me * T, T), :] = layer_norm(after[...], gains[3:4], shifts[3:4]).astype(bf16)
+    gd2.send(0)
+    save(after, o_as)
+
+    attend_block(mate, s1.put_mate)
+    attend_block(me, s1.put_own)
+    lt[...] = jnp.transpose(l[...])[0:8]
+    save(lt, o_l)
+    save(a, o_a)
+
+    ge2 = Gather(g2, ag2, R, S)
+
+    @pl.loop(0, steps)
+    def _(j):
+        part = window(j * S, S)
+        rows = enc_in[0, part, :].astype(f32) + s1.total(j) + branch_bias[0:1]
+        mid[part, :] = rows
+        g2[window(me * R + j * S, S), :] = layer_norm(rows, gains[1:2], shifts[1:2]).astype(bf16)
+        ge2.send(j)
+
+    save(mid, o_mid)
+    gd2.mate(0)
+    gd2.opp(0)
+    gd2.diag(0)
+    loads[2].wait()
+    cq[...] = (dot(m2[...], w_c[0]) + head_bias[2, 0:1]).astype(bf16)
+    save(m2, o_m2)
+    save(cq, o_cq)
+    loads[5].wait()
+    loads[6].wait()
+    s2 = Scatter(*rs2, R, S)
+
+    def feed(block, j):
+        part = window(block * R + j * S, S)
+        hidden = dot(g2[part, :], w_f1[...]) + wide_bias[0:1]
+        active, slope = gelu_parts(hidden)
+        active = active.astype(bf16)
+        e[part, :] = active
+        gd[part, :] = slope.astype(bf16)
+        return dot(active, w_f2[...])
+
+    @pl.loop(0, steps)
+    def _(j):
+        s2.put_own(j, feed(me, j))
+
+    @pl.loop(0, steps)
+    def _(j):
+        ge2.mate(j)
+        s2.put_mate(j, feed(mate, j))
+
+    @pl.loop(0, steps)
+    def _(j):
+        ge2.opp(j)
+        ge2.diag(j)
+        s2.put_diag(j, feed(diag, j))
+        s2.put_opp(j, feed(opp, j))
+
+    save(g2, o_g2)
+    save(e, o_e)
+    save(gd, o_gd)
+    ge3 = Gather(g3, ag3, R, S)
+
+    @pl.loop(0, steps)
+    def _(j):
+        part = window(j * S, S)
+        rows = (mid[part, :] + s2.total(j) + branch_bias[1:2]).astype(bf16)
+        enc[part, :] = rows
+        g3[window(me * R + j * S, S), :] = rows
+        ge3.send(j)
+
+    save(enc, o_enc)
+
+    def cross_block(block):
+        part = window(block * R, R)
+        rows = g3[part, :]
+        ck[part, :] = dot(rows, w_c[1]).astype(bf16)
+        cv[part, :] = (dot(rows, w_c[2]) + head_bias[2, 1:2]).astype(bf16)
+
+    @pl.loop(0, steps)
+    def _(j):
+        ge3.mate(j)
+
+    @pl.loop(0, 2)
+    def _(i):
+        cross_block(me + i * (mate - me))
+
+    @pl.loop(0, steps)
+    def _(j):
+        ge3.opp(j)
+
+    @pl.loop(0, steps)
+    def _(j):
+        ge3.diag(j)
+
+    @pl.loop(0, 2)
+    def _(i):
+        cross_block(opp + i * (diag - opp))
+
+    save(g3, o_g3)
+    save(ck, o_ck)
+    save(cv, o_cv)
+
+    @pl.loop(0, steps)
+    def _(j):
+        for each in (ge1, s1, ge2, s2, ge3):
+            each.close(j)
+
+    for each in (gd1, sd, gd2):
+        each.close(0)
+    for copy in saves:
+        copy.wait()
+
+
+def forward_call(enc_in, dec_in, norm_gain, norm_shift, qv_bias, out_bias, fc1_bias, qkv, proj, fc1, fc2):
+    R, D = enc_in.shape[1:]
+    T = dec_in.shape[1]
+    W = qkv.shape[-1]
+    F = fc1.shape[-1]
+    steps = R // T
+    V = lambda *shape: pltpu.VMEM(shape, bf16)
+    V32 = lambda *shape: pltpu.VMEM(shape, f32)
+    B = lambda *shape: jax.ShapeDtypeStruct(shape, bf16)
+    B32 = lambda *shape: jax.ShapeDtypeStruct(shape, f32)
+    N, M = 4 * R, 4 * T
+    outs = dict(
+        enc=B(R, D), g1=B(N, D), q=B(N, W), k=B(N, W), v=B(N, W), a=B(N, W), l=B32(8, N), mid=B32(R, D),
+        g2=B(N, D), e=B(N, F), gd=B(N, F), g3=B(N, D), ck=B(N, W), cv=B(N, W),
+        m1=B(M, D), sq=B(M, W), sk=B(M, W), sv=B(M, W), sa=B(M, W), sl=B32(8, M), after=B32(T, D),
+        m2=B(M, D), cq=B(M, W),
+    )
+    scratch = [
+        V(3, D, W), V(3, D, W), V(3, D, W), V(W, D), V(W, D), V(D, F), V(F, D),
+        V(N, D), V(N, W), V(N, W), V(N, W), V(N, W), V32(N, 128), V32(8, N), V32(R, D), V(N, D), V(N, F), V(N, F),
+        V(N, D), V(N, W), V(N, W),
+        V(M, D), V(M, W), V(M, W), V(M, W), V(M, W), V32(M, 128), V32(8, M), V32(T, D), V(M, D), V(M, W), V(R, D),
+    ]
+    scratch += scatter_shapes(R, D, steps) + scatter_shapes(R, D, steps) + scatter_shapes(T, D, 1)
+    scratch += [pltpu.SemaphoreType.DMA((6, steps))] * 3 + [pltpu.SemaphoreType.DMA((6, 1))] * 2
+    scratch += [pltpu.SemaphoreType.DMA((7,)), pltpu.SemaphoreType.DMA((len(outs),))]
+    results = pl.pallas_call(
+        functools.partial(forward_kernel, R, T),
+        out_shape=list(outs.values()),
+        in_specs=[VMEM] * 7 + [ANY] * 4,
+        out_specs=[ANY] * len(outs),
+        scratch_shapes=scratch,
+        compiler_params=pltpu.CompilerParams(
+            collective_id=0, has_side_effects=True, vmem_limit_bytes=60 << 20
+        ),
+        name="encoder_forward",
+    )(enc_in, dec_in, norm_gain, norm_shift, qv_bias, out_bias, fc1_bias, qkv, proj, fc1, fc2)
+    return dict(zip(outs, results))
 
 
 def normalize(rows_in, gain_row, shift_row):
@@ -188,7 +650,7 @@
     branch = gather_grads(gradient.astype(jnp.bfloat16))
     fc2_grad = weight_grad(activated, branch)
     bias_mlp = column_sums(branch)
-    hidden_grad = activate_back(hidden, product_back(branch, fc2[0])).astype(jnp.bfloat16)
+    hidden_grad = (hidden.astype(jnp.float32) * product_back(branch, fc2[0])).astype(jnp.bfloat16)
     fc1_grad = weight_grad(gathered_two, hidden_grad)
     fc1_bias_grad = column_sums(hidden_grad)
     middle_norm, gain_one, shift_one = norm_back(
@@ -236,20 +698,12 @@
     )
 
 
-def decoder_forward(tokens, memory, valid_rows, weights):
+def decoder_forward(tokens, memory, valid_rows, weights, kept, logs):
     norm_gain, norm_shift, qkv, qv_bias, proj, out_bias, fc1, fc1_bias, fc2 = weights
-    gathered = gather_rows(normalize(tokens, norm_gain[2], norm_shift[2]).astype(jnp.bfloat16))
-    queries = (product(gathered, qkv[1, 0]) + qv_bias[1, 0]).astype(jnp.bfloat16)
-    key_rows = product(gathered, qkv[1, 1]).astype(jnp.bfloat16)
-    values = (product(gathered, qkv[1, 2]) + qv_bias[1, 1]).astype(jnp.bfloat16)
-    mixed_out, logsum = attend(queries, key_rows, values, True)
-    after_self = tokens + sum_rows(product(mixed_out, proj[1])) + out_bias[2]
-    gathered_two = gather_rows(
-        normalize(after_self, norm_gain[3], norm_shift[3]).astype(jnp.bfloat16)
-    )
-    cross_queries = (product(gathered_two, qkv[2, 0]) + qv_bias[2, 0]).astype(jnp.bfloat16)
-    cross_keys = product(memory, qkv[2, 1]).astype(jnp.bfloat16)
-    cross_values = (product(memory, qkv[2, 2]) + qv_bias[2, 1]).astype(jnp.bfloat16)
+    gathered, queries, key_rows, values, mixed_out = (kept[n][None] for n in ("m1", "sq", "sk", "sv", "sa"))
+    logsum = logs(kept["sl"])
+    after_self = kept["after"][None]
+    gathered_two, cross_queries, cross_keys, cross_values = (kept[n][None] for n in ("m2", "cq", "ck", "cv"))
     cross_mixed, cross_logsum = attend(cross_queries, cross_keys, cross_values, False)
     second = after_self + sum_rows(product(cross_mixed, proj[2])) + out_bias[3]
     gathered_three = gather_rows(
@@ -412,10 +866,14 @@
         jnp.int32, (clip_count, token_count), 1
     )
     valid_rows = (positions < dec_len[:, None]).astype(jnp.float32)[:, :, None]
-    encoded, enc_saved = encoder_forward(frames, weights)
-    enc_out = encoded.astype(jnp.bfloat16)
-    memory = gather_rows(enc_out)
-    decoded, dec_saved = decoder_forward(tokens, memory, valid_rows, weights)
+    kept = forward_call(enc_in, dec_in, norm_gain, norm_shift, qv_bias, out_bias, fc1_bias, qkv, proj, fc1, fc2)
+    enc_out = kept["enc"][None]
+    memory = kept["g3"][None]
+    ln2 = math.log(2.0)
+    logs = lambda t: (t[:3] * ln2)[None, :, :, None]
+    enc_saved = (kept["g1"][None], kept["q"][None], kept["k"][None], kept["v"][None], kept["a"][None], logs(kept["l"]),
+        kept["mid"][None], kept["g2"][None], kept["gd"][None], kept["e"][None])
+    decoded, dec_saved = decoder_forward(tokens, memory, valid_rows, weights, kept, logs)
     tokens_grad, memory_grad, dec_grads, dec_gains, dec_shifts = decoder_backward(
         tokens, memory, dec_saved, dec_cot.astype(jnp.float32) * valid_rows, weights
     )

time: 911 us -> 786 us (0.86)
  waiting for transfers between devices: 463 us -> 329 us
  Pallas kernels: 0 us -> 84.1 us
  matrix products: 180 us -> 135 us
  other arithmetic: 88.3 us -> 68.6 us
  blocking collectives: 129 us -> 114 us
    pallas_call x0 -> x1, Pallas kernels: none -> 84.1 us  [forward_call(): pl.pallas_call(functools.partial(forward_kernel, R, T), out_shape=list(ou...]
    reduce_scatter x5 -> x2, waiting for transfers between devices: 106 us -> 34.6 us  [sum_rows(): lax.psum_scatter(partial_value.astype(jnp.bfloat16), 'mp', scatter_dimens...]
    all_gather x3 -> x0, waiting for transfers between devices: 58.2 us -> none  [gather_rows(): return lax.all_gather(normed, 'mp', axis=1, tiled=True)]
    dot_general x16 -> x3, matrix products: 46.9 us -> 10.1 us  [product(): jnp.einsum('crd,dh->crh', operand, weight, preferred_element_type=jnp.flo...]
    all_gather x3 -> x1, blocking collectives: 23.6 us -> 7.66 us  [gather_rows(): return lax.all_gather(normed, 'mp', axis=1, tiled=True)]
    dot_general x3, matrix products: 5.06 us -> 20.7 us  [score_block(): jnp.einsum('rhe,she->hrs', split_query, split_keys, preferred_element_typ...]
    dot_general x3 -> x1, matrix products: 13.4 us -> 1.52 us  [one_clip(): jnp.einsum('hrs,she->rhe', weights, split_values, preferred_element_type=...]
    reduce_scatter x6, waiting for transfers between devices: 92.7 us -> 83.2 us  [sum_grads(): lax.psum_scatter(partial_value.astype(jnp.bfloat16), 'mp', scatter_dimens...]
  transfers between devices with their start and end apart: 17 -> 11, of which waited for: 15 -> 9; matrix products, arithmetic and copies ran while one was open for 17% -> 20% of each run, Pallas kernels for 0% -> 0%
where the time goes in v2:
time: 786 us; the launch traced here: 776 us
  waiting for transfers between devices  329 us (42%)
  matrix products  135 us (17%)
  blocking collectives  114 us (15%)
  Pallas kernels  84.1 us (11%)
  other arithmetic  68.6 us (9%)
  local copies, waits for them, and re-layouts  28.3 us (4%)
  between operations  16.5 us (2%)
    psum x1, waiting for transfers between devices, sum_clips(): return tuple((value.astype(jnp.float32) for value in lax.psum(sent, 'dp')))  192 us
    pallas_call x1, Pallas kernels, forward_call(): pl.pallas_call(functools.partial(forward_kernel, R, T), out_shape=list(ou...  84.1 us
    reduce_scatter x6, waiting for transfers between devices, sum_grads(): lax.psum_scatter(partial_value.astype(jnp.bfloat16), 'mp', scatter_dimens...  83.2 us
    psum x1, blocking collectives, on_device(): lax.psum((jnp.concatenate([enc_gains, dec_gains]), jnp.concatenate([enc_s...  42.1 us
    psum x1, blocking collectives, on_device(): narrow = lax.psum((merged[1], merged[3], merged[5]), 'dp')  40.1 us
    dot_general x16, matrix products, product_back(): jnp.einsum('crh,dh->crd', gradient, weight, preferred_element_type=jnp.fl...  38.9 us
    reduce_scatter x2, waiting for transfers between devices, sum_rows(): lax.psum_scatter(partial_value.astype(jnp.bfloat16), 'mp', scatter_dimens...  34.6 us
    all_gather x3, blocking collectives, gather_grads(): return lax.all_gather(gradient, 'mp', axis=1, tiled=True)  24.2 us
  transfers between devices with their start and end apart: 11, of which 9 were waited for; matrix products, arithmetic and copies ran while one was open for 20% of the time, Pallas kernels for 0%

profile of v2, /device:TPU:0, one launch (start us, length us, event | category | flops | bytes accessed | tf_op | source)
XLA Modules:
  0.0 776.2 jit_solution(1564660038877757845)
XLA Ops:
  7.2 5.7 copy.50.qkv
  13.0 84.1 %encoder_forward.1 = (bf16[336,768]{1,0:T(8,128)(2,1)}, bf16[1344,768]{1,0:T(8,128)(2,1)}, bf16[1344,192]{1,0:T(8,128)(2,1)}, bf16[1344,192]{1,0:T(8,128)(2,1)},...) custom-call(bf16[1,336,768]{2,1,0:T(8,128)(2,1)} %enc_in.1, ...), custom_call_target="tpu_custom_call" | custom-call | tf_op jit(solution)/shard_map/encoder_forward/pallas_call | solution.py:461
  111.3 8.7 %all_gather.19 = bf16[1,448,768]{2,1,0:T(8,128)(2,1)S(1)} all-gather(bf16[1,112,768]{2,1,0:T(8,128)(2,1)S(1)} %fusion.120), channel_id=1, replica_groups=mesh['dp'=8,'mp'=4] {'mp'}, dimensions={1}, use_global_device_ids=true | all-gather | bytes 860160 | tf_op jit(solution)/shard_map/all_gather | solution.py:523
  119.9 11.8 %reduce-scatter.9.cloned.1.call-done = bf16[1,112,768]{2,1,0:T(8,128)(2,1)} async-done(((bf16[1,448,768]{2,1,0:T(8,128)(2,1)}), bf16[1,112,768]{2,1,0:T(8,128)(2,1)}) %reduce-scatter.9.cloned.1.call-update) | async-done | bytes 172048 | tf_op jit(solution)/shard_map/reduce_scatter | solution.py:517
  133.7 7.7 all_gather.18
  141.3 4.6 multiply_convert_fusion.4
  153.5 19.9 %reduce-scatter.13.cloned.1.call-done = bf16[1,112,768]{2,1,0:T(8,128)(2,1)} async-done(((bf16[1,448,768]{2,1,0:T(8,128)(2,1)}), bf16[1,112,768]{2,1,0:T(8,128)(2,1)}) %reduce-scatter.13.cloned.1.call-update) | async-done | bytes 172048 | tf_op jit(solution)/shard_map/reduce_scatter | solution.py:527
  176.3 22.9 %reduce-scatter.11.cloned.1.call-done = bf16[1,112,768]{2,1,0:T(8,128)(2,1)} async-done(((bf16[1,448,768]{2,1,0:T(8,128)(2,1)}), bf16[1,112,768]{2,1,0:T(8,128)(2,1)}) %reduce-scatter.11.cloned.1.call-update) | async-done | bytes 172048 | tf_op jit(solution)/shard_map/reduce_scatter | solution.py:517
  202.6 7.7 all_gather.20
  212.7 5.4 convert_reduce_fusion.10
  229.5 31.7 %reduce-scatter.15.cloned.1.call-done = bf16[1,336,768]{2,1,0:T(8,128)(2,1)} async-done(((bf16[1,1344,768]{2,1,0:T(8,128)(2,1)}), bf16[1,336,768]{2,1,0:T(8,128)(2,1)}) %reduce-scatter.15.cloned.1.call-update) | async-done | bytes 516112 | tf_op jit(solution)/shard_map/reduce_scatter | solution.py:527
  263.4 4.1 convert_reduce_fusion.17
  269.8 15.9 %all-gather.3.cloned.1.call-done = bf16[1,1344,768]{2,1,0:T(8,128)(2,1)} async-done(((bf16[1,336,768]{2,1,0:T(8,128)(2,1)}), bf16[1,1344,768]{2,1,0:T(8,128)(2,1)}) %all-gather.3.cloned.1.call-update) | async-done | bytes 2064400 | tf_op jit(solution)/shard_map/all_gather | solution.py:523
  285.7 4.8 convert_reduce_fusion
  316.8 29.3 %reduce-scatter.17.cloned.1.call-done = bf16[1,336,768]{2,1,0:T(8,128)(2,1)} async-done(((bf16[1,1344,768]{2,1,0:T(8,128)(2,1)}), bf16[1,336,768]{2,1,0:T(8,128)(2,1)}) %reduce-scatter.17.cloned.1.call-update) | async-done | bytes 516112 | tf_op jit(solution)/shard_map/reduce_scatter | solution.py:527
  350.9 7.9 %all_gather.23 = bf16[1,448,768]{2,1,0:T(8,128)(2,1)S(1)} all-gather(bf16[1,112,768]{2,1,0:T(8,128)(2,1)S(1)} %copy-done.71), channel_id=1, replica_groups=mesh['dp'=8,'mp'=4] {'mp'}, dimensions={1}, use_global_device_ids=true | all-gather | bytes 860160 | tf_op jit(solution)/shard_map/all_gather | solution.py:523
  376.0 11.0 %fusion.168 = f32[3,1344,1344]{1,2,0:T(8,128)} fusion(bf16[1344,3,64]{0,2,1:T(8,128)(2,1)S(1)} %bitcast.329, bf16[1344,3,64]{0,2,1:T(8,128)(2,1)S(1)} %bitcast.331), kind=kOutput, calls=%fused_computation.306 | convolution fusion | flops 693633024 | bytes 22708224 | tf_op jit(solution)/shard_map/while/body/eval_jaxpr/rhe,she->hrs/dot_general | solution.py:576
  387.0 18.5 %multiply_reduce_fusion = (f32[3,1344]{1,0:T(4,128)S(1)}, f32[3,1344,1344]{1,2,0:T(8,128)}) fusion(f32[3,1344,1344]{1,2,0:T(8,128)} %fusion.168, f32[3,1344]{1,0:T(4,128)S(1)} %copy-done.73, bf16[1344,3,64]{0,2,1:T(8,128)(2,1)S(1)} %bitcast.313, bf16[1344,3,64]{0,2,1:T(8,128)(2,1)S(1)} %bitcast.309), kind=kOutput, calls=%fused_computation.1 | convolution fusion | flops 715305024 | bytes 44416512 | tf_op jit(solution)/shard_map/while/body/eval_jaxpr/rhe,she->hrs/dot_general | solution.py:541
  405.5 14.6 %multiply_convert_fusion = bf16[3,1344,1344]{1,2,0:T(8,128)(2,1)S(1)} fusion(f32[3,1344,1344]{1,2,0:T(8,128)} %get-tuple-element.221, f32[3,1344,1344]{1,2,0:T(8,128)} %fusion.168, f32[3,1344]{1,0:T(4,128)S(1)} %get-tuple-element.220), kind=kLoop, calls=%fused_computation | loop fusion | flops 16257024 | bytes 54206208 | tf_op jit(solution)/shard_map/while/body/eval_jaxpr/convert_element_type | solution.py:580
  431.0 11.1 %convert_reduce_fusion.11 = (f32[3,64]{1,0:T(4,128)S(1)}, bf16[3,64,1344]{2,1,0:T(8,128)(2,1)S(1)}) fusion(bf16[1344,3,64]{0,2,1:T(8,128)(2,1)} %bitcast.330, f32[3,1344,1344]{1,2,0:T(8,128)} %get-tuple-element.221), kind=kOutput, calls=%fused_computation.149 | convolution fusion | flops 699825984 | bytes 22708992 | tf_op jit(solution)/shard_map/while/body/eval_jaxpr/hrs,rhe->she/dot_general | solution.py:590
  442.1 4.7 fusion.3
  479.4 40.1 %all-reduce.1 = (f32[3,2,192]{2,1,0:T(2,128)}, f32[5,768]{1,0:T(8,128)}, f32[2,768]{1,0:T(2,128)}) all-reduce(f32[3,2,192]{2,1,0:T(2,128)S(1)} %pad_maximum_fusion.2, f32[5,768]{1,0:T(8,128)S(1)} %concatenate.31, f32[2,768]{1,0:T(2,128)S(1)} %pad_maximum_fusion.3), channel_id=1, replica_groups=mesh['dp'=8,'mp'=4] {'dp'}, use_global_device_ids=true, to_apply=%region_53.54 | all-reduce | flops 6528 | bytes 52224 | tf_op jit(solution)/shard_map/psum | solution.py:896
  523.0 42.1 %all-reduce = (f32[5,768]{1,0:T(8,128)}, f32[5,768]{1,0:T(8,128)}) all-reduce(f32[5,768]{1,0:T(8,128)S(1)} %concatenate.24, f32[5,768]{1,0:T(8,128)S(1)} %concatenate.25), channel_id=1, replica_groups=mesh['dp'=8,'mp'=4] {'dp','mp'}, use_global_device_ids=true, to_apply=%region_38.39 | all-reduce | flops 7680 | bytes 61440 | tf_op jit(solution)/shard_map/psum | solution.py:898
  566.7 191.5 %all-reduce.5.cloned.1.call-done = (bf16[2,3,768,192]{2,3,1,0:T(8,128)(2,1)}, bf16[1,3,768,192]{2,3,1,0:T(8,128)(2,1)}, bf16[2,192,768]{2,1,0:T(8,128)(2,1)}, bf...) async-done(((bf16[2,3,768,192]{2,3,1,0:T(8,128)(2,1)}, ...) | async-done | bytes 8257552 | tf_op jit(solution)/shard_map/psum | solution.py:534
  (411 shorter events, 153.9 us)
Async XLA Ops:
  7.2 124.5 %reduce-scatter.9.cloned.1.call-start = ((), (), s32[]{:S(2)}) async-start(), calls=%async_computation.8 | async-start | bytes 860160 | tf_op jit(solution)/shard_map/reduce_scatter | solution.py:517
  108.2 33.1 %copy-start.41 = (bf16[2,768,768]{2,1,0:T(8,128)(2,1)S(1)}, bf16[2,768,768]{2,1,0:T(8,128)(2,1)}, u32[]{:S(2)}) copy-start(bf16[2,768,768]{2,1,0:T(8,128)(2,1)} %fc1.1) | copy-start | bytes 7077892
  108.2 65.1 %reduce-scatter.13.cloned.1.call-start = ((), (), s32[]{:S(2)}) async-start(), calls=%async_computation.10 | async-start | bytes 860160 | tf_op jit(solution)/shard_map/reduce_scatter | solution.py:527
  109.1 36.8 %copy-start.95 = (f32[112]{0:T(128)}, f32[112]{0:T(128)S(1)}, u32[]{:S(2)}) copy-start(f32[112]{0:T(128)S(1)} %compare_convert_fusion) | copy-start | bytes 1348
  111.2 34.8 %copy-start.80 = (f32[768]{0:T(1024)}, f32[768]{0:T(1024)S(1)}, u32[]{:S(2)}) copy-start(f32[768]{0:T(1024)S(1)} %get-tuple-element.182) | copy-start | bytes 9220
  150.1 49.0 %reduce-scatter.11.cloned.1.call-start = ((), (), s32[]{:S(2)}) async-start(), calls=%async_computation.9 | async-start | bytes 860160 | tf_op jit(solution)/shard_map/reduce_scatter | solution.py:517
  150.2 51.8 %copy-start.59 = (bf16[1,112,768]{2,1,0:T(8,128)(2,1)S(1)}, bf16[1,112,768]{2,1,0:T(8,128)(2,1)}, u32[]{:S(2)}) copy-start(bf16[1,112,768]{2,1,0:T(8,128)(2,1)} %param.27) | copy-start | bytes 516100
  150.2 67.9 %slice-start = ((s8[7569408]{0:T(1024)(128)(4,1)}), s8[3375104]{0:T(1024)(128)(4,1)S(1)}, s32[]{:S(2)}) async-start(s8[7569408]{0:T(1024)(128)(4,1)} %bitcast.307), calls=%async_computation.19 | async-start | bytes 6750208
  153.4 107.8 %reduce-scatter.15.cloned.1.call-start = ((), (), s32[]{:S(2)}) async-start(), calls=%async_computation.11 | async-start | bytes 2580480 | tf_op jit(solution)/shard_map/reduce_scatter | solution.py:527
  229.4 31.8 %copy-start.28 = (bf16[1,336,768]{2,1,0:T(8,128)(2,1)S(1)}, bf16[1,336,768]{2,1,0:T(8,128)(2,1)}, u32[]{:S(2)}) copy-start(bf16[1,336,768]{2,1,0:T(8,128)(2,1)} %param.26) | copy-start | bytes 1548292
  229.4 34.0 %copy-start.23 = (bf16[1344,192]{0,1:T(8,128)(2,1)S(1)}, bf16[1344,192]{0,1:T(8,128)(2,1)}, u32[]{:S(2)}) copy-start(bf16[1344,192]{0,1:T(8,128)(2,1)} %copy-done.22) | copy-start | bytes 1548292
  229.4 56.3 %all-gather.3.cloned.1.call-start = ((), (), s32[]{:S(2)}) async-start(), calls=%async_computation.12 | async-start | bytes 2580480 | tf_op jit(solution)/shard_map/all_gather | solution.py:523
  263.2 48.3 %reduce-scatter.21.cloned.1.call-start = ((), (), s32[]{:S(2)}) async-start(), calls=%async_computation.16 | async-start | bytes 860160 | tf_op jit(solution)/shard_map/reduce_scatter | solution.py:527
  269.7 76.4 %reduce-scatter.17.cloned.1.call-start = ((), (), s32[]{:S(2)}) async-start(), calls=%async_computation.13 | async-start | bytes 2580480 | tf_op jit(solution)/shard_map/reduce_scatter | solution.py:527
  295.0 78.4 %all-gather.5.cloned.1.call-start = ((), (), s32[]{:S(2)}) async-start(), calls=%async_computation.14 | async-start | bytes 2580480 | tf_op jit(solution)/shard_map/all_gather | solution.py:523
  303.4 42.7 %copy-start.85 = (f32[336]{0:T(512)}, f32[336]{0:T(512)S(1)}, u32[]{:S(2)}) copy-start(f32[336]{0:T(512)S(1)} %fusion.154) | copy-start | bytes 4036
  309.2 36.9 %copy-start.83 = (f32[768]{0:T(1024)S(1)}, f32[768]{0:T(1024)}, u32[]{:S(2)}) copy-start(f32[768]{0:T(1024)} %get-tuple-element.181) | copy-start | bytes 9220
  350.9 121.3 %reduce-scatter.23.cloned.1.call-start = ((), (), s32[]{:S(2)}) async-start(), calls=%async_computation.17 | async-start | bytes 860160 | tf_op jit(solution)/shard_map/reduce_scatter | solution.py:527
  369.9 149.6 %reduce-scatter.19.cloned.1.call-start = ((), (), s32[]{:S(2)}) async-start(), calls=%async_computation.15 | async-start | bytes 2580480 | tf_op jit(solution)/shard_map/reduce_scatter | solution.py:527
  446.7 311.5 %all-reduce.5.cloned.1.call-start = ((), (), s32[]{:S(2)}) async-start(), calls=%async_computation.18 | async-start | bytes 16515072 | tf_op jit(solution)/shard_map/psum | solution.py:534
  476.7 42.8 %copy-start.81 = (f32[768]{0:T(1024)S(1)}, f32[768]{0:T(1024)}, u32[]{:S(2)}) copy-start(f32[768]{0:T(1024)} %get-tuple-element.180) | copy-start | bytes 9220
  478.8 86.3 %copy-start.30 = (bf16[1,336,768]{2,1,0:T(8,128)(2,1)S(1)}, bf16[1,336,768]{2,1,0:T(8,128)(2,1)}, u32[]{:S(2)}) copy-start(bf16[1,336,768]{2,1,0:T(8,128)(2,1)} %param.26) | copy-start | bytes 1548292
  478.8 86.3 %copy-start.32 = (bf16[1,336,768]{2,1,0:T(8,128)(2,1)S(1)}, bf16[1,336,768]{2,1,0:T(8,128)(2,1)}, u32[]{:S(2)}) copy-start(bf16[1,336,768]{2,1,0:T(8,128)(2,1)} %reduce-scatter.15.cloned.1.call-done) | copy-start | bytes 1548292
  519.5 45.6 %copy-start.33 = (bf16[1,336,768]{2,1,0:T(8,128)(2,1)S(1)}, bf16[1,336,768]{2,1,0:T(8,128)(2,1)}, u32[]{:S(2)}) copy-start(bf16[1,336,768]{2,1,0:T(8,128)(2,1)} %reduce-scatter.19.cloned.1.call-done) | copy-start | bytes 1548292
  (103 other events, 463.3 us)
Sparse Core Ops, SparseCore 0:
  108.3 23.3 reduce-scatter.8
  150.3 23.0 reduce-scatter.12
  176.5 22.6 reduce-scatter.10
  229.6 31.5 reduce-scatter.14
  263.3 22.3 all-gather.2
  288.8 22.6 reduce-scatter.20
  314.9 31.1 reduce-scatter.16
  351.0 22.4 all-gather.4
  376.6 22.6 reduce-scatter.22
  446.9 31.2 reduce-scatter.18
  485.5 272.6 all-reduce.4
